TPU v7x, 256 devices: a whole 4x4x8 slice. The times are simulated.
256 devices in a mesh: dp: 16 (over y_hi, x, core), seq: 16 (over z, y_lo).
Axes of the slice: x: 4, y: 4 (y_hi: 2, y_lo: 2; y = y_hi * 2 + y_lo), z: 8, core: 2. Of those that a mesh axis runs over, the one named last changes fastest.
Arguments:
- qkv: bfloat16 [2, 32768, 3, 2048], P(None, ('dp', 'seq')), may hold values from -100 to 100
- cotangent: bfloat16 [2, 32768, 1536], P(None, ('dp', 'seq')), may hold values from -6 to 6
- out_weight: bfloat16 [2048, 1536], P(('seq', 'dp')), may hold values from -0.125 to 0.125
- gate_table: float32 [50, 1536], replicated, may hold values from 0.25 to 2
- timestep: int32 [16], P('dp'), may hold values from 1 to 49
- plan: int32 [16, 16], P('dp'), may hold values from 0 to 1, as said below
Outputs:
- qkv_grad: bfloat16 [2, 32768, 3, 2048], P(None, ('dp', 'seq'))
- weight_grad: float32 [2048, 1536], P(('seq', 'dp'))
Inputs may be any that keep to these rules, and one draw needn't show every extreme that they name: `plan`: in each clip exactly 12 frames are 1, the others 0.
All inputs are finite; a program needn't handle non-finite values.
Results may differ from a plain program's by a relative error of at most 0.034.
Values may be sent and summed in bfloat16 or wider, within the bound.
No kernel may reach another device: no remote copies, remote signals or barrier semaphores. Data moves between devices by JAX's collectives and lax.ppermute only.
A program may use at most 128 MiB of HBM per device.

v0:
```python
import jax
import jax.numpy as jnp
from jax import lax
from jax.sharding import PartitionSpec as P

HEAD_DIM = 64
FT = 128


def block_rows(frame_count):
    best = 1
    for size in range(1, frame_count + 1):
        if frame_count % size == 0 and size * FT <= 512:
            best = size
    return best * FT


def pick_frames(field, live, every_frame):
    shaped = field.reshape((every_frame, FT) + field.shape[1:])
    return shaped[live].reshape((live.shape[0] * FT,) + field.shape[1:])


def place_frames(field, live, every_frame):
    shaped = field.reshape((live.shape[0], FT) + field.shape[1:])
    empty = jnp.zeros((every_frame, FT) + field.shape[1:], field.dtype)
    return empty.at[live].set(shaped).reshape((every_frame * FT,) + field.shape[1:])


def attend(rows_q, keys, values, rows_grad, scale):
    count, heads_here, depth = rows_q.shape
    block = block_rows(count // FT)
    blocks = count // block
    zeros = jnp.zeros(keys.shape, jnp.float32)

    def one_block(carry, pair):
        dk_acc, dv_acc = carry
        query_b, grad_b = pair
        scores = (
            jnp.einsum("qhd,khd->hqk", query_b, keys, preferred_element_type=jnp.float32) * scale
        )
        top = jnp.max(scores, axis=2, keepdims=True)
        expo = jnp.exp(scores - top)
        probs = expo / jnp.sum(expo, axis=2, keepdims=True)
        probs_low = probs.astype(jnp.bfloat16)
        output = jnp.einsum(
            "hqk,khd->qhd", probs_low, values, preferred_element_type=jnp.float32
        ).astype(jnp.bfloat16)
        grad_probs = jnp.einsum("qhd,khd->hqk", grad_b, values, preferred_element_type=jnp.float32)
        delta = jnp.sum(grad_b.astype(jnp.float32) * output.astype(jnp.float32), axis=2)
        grad_scores = (probs * (grad_probs - jnp.transpose(delta)[:, :, None])).astype(jnp.bfloat16)
        grad_q = (
            jnp.einsum("hqk,khd->qhd", grad_scores, keys, preferred_element_type=jnp.float32)
            * scale
        ).astype(jnp.bfloat16)
        dk_acc = dk_acc + jnp.einsum(
            "hqk,qhd->khd", grad_scores, query_b, preferred_element_type=jnp.float32
        )
        dv_acc = dv_acc + jnp.einsum(
            "hqk,qhd->khd", probs_low, grad_b, preferred_element_type=jnp.float32
        )
        return ((dk_acc, dv_acc), (output, grad_q))

    inputs = (
        rows_q.reshape(blocks, block, heads_here, depth),
        rows_grad.reshape(blocks, block, heads_here, depth),
    )
    (dk_acc, dv_acc), (outputs, grad_q) = lax.scan(one_block, (zeros, zeros), inputs)
    width = heads_here * depth
    grad_k = (dk_acc * scale).astype(jnp.bfloat16).reshape(-1, width)
    grad_v = dv_acc.astype(jnp.bfloat16).reshape(-1, width)
    return (outputs.reshape(count, width), grad_q.reshape(count, width), grad_k, grad_v)


def per_device(qkv, cotangent, out_weight, gate_table, timestep, plan):
    scale = HEAD_DIM ** (-0.5)
    token_rows = qkv.shape[1]
    n_seq = lax.axis_size("seq")
    seq_pos = lax.axis_index("seq")
    frames_here = token_rows // FT
    every_frame = frames_here * n_seq
    live_count = every_frame // 4
    gate_now = lax.dynamic_index_in_dim(gate_table, timestep[0], 0, keepdims=False)
    gate_prev = lax.dynamic_index_in_dim(gate_table, timestep[0] - 1, 0, keepdims=False)
    flags = plan[0]
    local_flags = lax.dynamic_slice_in_dim(flags, seq_pos * frames_here, frames_here)
    reuse = jnp.repeat(local_flags, FT).astype(jnp.float32)[:, None]
    grads_in = cotangent.astype(jnp.float32)
    res_one = (gate_now * grads_in[0] + reuse * (gate_prev * grads_in[1])).astype(jnp.bfloat16)
    res_two = ((1.0 - reuse) * (gate_prev * grads_in[1])).astype(jnp.bfloat16)
    residual_gradient = jnp.stack([res_one, res_two])
    live = jnp.argsort(flags, stable=True)[:live_count]
    weight_group = lax.all_gather(out_weight, "dp", axis=0, tiled=True)
    grad_out = jnp.einsum(
        "tze,ke->tzk",
        residual_gradient,
        lax.all_gather(weight_group, "seq", axis=0, tiled=True),
        preferred_element_type=jnp.float32,
    ).astype(jnp.bfloat16)
    grads_tok = []
    outputs_kept = []
    for step in range(2):
        heads, grad_heads = (
            lax.all_to_all(qkv[step], "seq", split_axis=2, concat_axis=0, tiled=True),
            lax.all_to_all(
                grad_out[step][:, None, :], "seq", split_axis=2, concat_axis=0, tiled=True
            ),
        )
        grad_heads = grad_heads[:, 0]
        length = heads.shape[0]
        heads_here = heads.shape[2] // HEAD_DIM
        queries = heads[:, 0].reshape(length, heads_here, HEAD_DIM)
        keys = heads[:, 1].reshape(length, heads_here, HEAD_DIM)
        values = heads[:, 2].reshape(length, heads_here, HEAD_DIM)
        grad_rows = grad_heads.reshape(length, heads_here, HEAD_DIM)
        if step == 0:
            outputs, grad_q, grad_k, grad_v = attend(queries, keys, values, grad_rows, scale)
        else:
            picked_q = pick_frames(queries, live, every_frame)
            picked_grad = pick_frames(grad_rows, live, every_frame)
            outputs_live, grad_live, grad_k, grad_v = attend(
                picked_q, keys, values, picked_grad, scale
            )
            outputs = place_frames(outputs_live, live, every_frame)
            grad_q = place_frames(grad_live, live, every_frame)
        grads = jnp.stack([grad_q, grad_k, grad_v], axis=1)
        returned, outputs_back = (
            lax.all_to_all(grads, "seq", split_axis=0, concat_axis=2, tiled=True),
            lax.all_to_all(outputs[:, None, :], "seq", split_axis=0, concat_axis=2, tiled=True),
        )
        outputs_kept.append(outputs_back[:, 0])
        grads_tok.append(returned)
    output_every = jnp.stack(outputs_kept)
    group_part = lax.psum_scatter(
        jnp.einsum(
            "vpt,vpg->tg", output_every, residual_gradient, preferred_element_type=jnp.float32
        ),
        "seq",
        scatter_dimension=0,
        tiled=True,
    )
    weight_grad = lax.psum_scatter(group_part, "dp", scatter_dimension=0, tiled=True)
    return (jnp.stack(grads_tok), weight_grad)


def solution(mesh):
    placed = (
        P(None, ("dp", "seq"), None, None),
        P(None, ("dp", "seq"), None),
        P(("seq", "dp"), None),
        P(),
        P("dp"),
        P("dp", None),
    )
    return jax.shard_map(
        per_device,
        mesh=mesh,
        in_specs=placed,
        out_specs=(P(None, ("dp", "seq"), None, None), P(("seq", "dp"), None)),
        check_vma=False,
    )
```

profile of v0, /device:TPU:2, one launch (start us, length us, event | category | flops | bytes accessed | tf_op | source)
XLA Modules:
  0.0 882.4 jit_solution(11323420986578158402)
XLA Ops:
  7.2 23.9 %all_gather.6 = bf16[128,1536]{1,0:T(8,128)(2,1)} all-gather(bf16[8,1536]{1,0:T(8,128)(2,1)} %param.10), channel_id=1, replica_groups=mesh['dp'=16,'seq'=16] {'dp'}, dimensions={0}, use_global_device_ids=true | all-gather | bytes 417792 | tf_op jit(solution)/shard_map/all_gather | solution.py:92
  37.1 7.8 all-to-all-start
  49.2 63.2 %all-to-all-done = bf16[128,3,2048]{0,1,2:T(4,128)(2,1)S(1)} async-done(((bf16[128,3,2048]{0,1,2:T(4,128)(2,1)}), bf16[128,3,2048]{0,1,2:T(4,128)(2,1)S(1)}, u32[]{:S(2)}, u32[]{:S(2)}) %all-to-all-start) | async-done | bytes 1572896 | tf_op jit(solution)/shard_map/all_to_all | solution.py:103
  112.4 12.6 %all-to-all-start.3 = ((bf16[128,3,2048]{0,1,2:T(4,128)(2,1)}), bf16[128,3,2048]{0,1,2:T(4,128)(2,1)}, u32[]{:S(2)}, u32[]{:S(2)}) async-start(bf16[128,3,2048]{0,1,2:T(4,128)(2,1)} %bitcast.16), calls=%async_computation.3 | async-start | bytes 4194304 | tf_op jit(solution)/shard_map/all_to_all | solution.py:103
  140.5 89.0 %all-gather.2.cloned.1.call-done = bf16[2048,1536]{1,0:T(8,128)(2,1)} async-done(((bf16[128,1536]{1,0:T(8,128)(2,1)}), bf16[2048,1536]{1,0:T(8,128)(2,1)}) %all-gather.2.cloned.1.call-update) | async-done | bytes 6291472 | tf_op jit(solution)/shard_map/all_gather | solution.py:96
  238.1 12.4 %reduce.5 = bf16[2048,128]{1,0:T(8,128)(2,1)} reduce(bf16[2048,1,128]{2,1,0:T(2,128)(2,1)S(1)} %bitcast.254, bf16[]{:T(256)} %broadcast.135), dimensions={1}, to_apply=%bitcast.150.reduce_sub_computation | reduce | bytes 1048578
  252.4 10.7 %all-to-all-start.1 = ((bf16[16,2,8192]{2,1,0:T(2,128)(2,1)}), bf16[16,2,8192]{2,1,0:T(2,128)(2,1)}, u32[]{:S(2)}, u32[]{:S(2)}) async-start(bf16[16,2,8192]{2,1,0:T(2,128)(2,1)} %reshape.96), calls=%async_computation.1 | async-start | bytes 1048576 | tf_op jit(solution)/shard_map/all_to_all | solution.py:104
  282.6 6.8 fusion.88
  293.0 13.4 %reduce.4 = bf16[2048,128]{1,0:T(8,128)(2,1)} reduce(bf16[2048,1,128]{2,1,0:T(2,128)(2,1)} %bitcast.255, bf16[]{:T(256)} %broadcast.135), dimensions={1}, to_apply=%bitcast.148.reduce_sub_computation | reduce | bytes 1048578
  308.3 8.5 all-to-all-start.4
  326.7 80.9 %while.3 = (s32[]{:T(128)}, f32[2048,2,64]{0,2,1:T(8,128)S(1)}, f32[2048,2,64]{0,2,1:T(8,128)S(1)}, bf16[4,512,2,64]{1,3,2,0:T(8,128)(2,1)}, bf16[4,512,2,64]{1,...) while((s32[]{:T(128)}, f32[2048,2,64]{0,2,1:T(8,128)S(1)}, ...), condition=%wide.region_4.5_spmd.clone, body=%wide.region_0.4_spmd.clone.sunk | while | flops 1630995456 | bytes 85086448 | solution.py:67
  326.7 6.6 fusion.147
  333.3 4.8 fusion.148
  346.9 6.6 fusion.147
  353.6 4.8 fusion.148
  367.2 6.6 fusion.147
  373.8 4.8 fusion.148
  387.4 6.6 fusion.147
  394.0 4.8 fusion.148
  411.9 13.0 %reduce.7 = bf16[2048,128]{1,0:T(8,128)(2,1)S(1)} reduce(bf16[2048,1,128]{2,1,0:T(2,128)(2,1)} %reshape.91, bf16[]{:T(256)} %broadcast.135), dimensions={1}, to_apply=%reshape.91.reduce_sub_computation | reduce | bytes 1048578 | tf_op jit(solution)/shard_map/broadcast_in_dim;reshape | solution.py:128
  425.8 8.3 all-to-all-start.6
  434.1 6.6 fusion.45
  452.0 8.1 all-to-all-start.7
  465.4 9.2 %all-to-all-done.7 = bf16[16,2,8192]{2,1,0:T(2,128)(2,1)} async-done(((bf16[16,2,8192]{2,1,0:T(2,128)(2,1)}), bf16[16,2,8192]{2,1,0:T(2,128)(2,1)}, u32[]{:S(2)}, u32[]{:S(2)}) %all-to-all-start.7) | async-done | bytes 524320 | tf_op jit(solution)/shard_map/all_to_all | solution.py:128
  479.0 7.7 convolution_bitcast_fusion.2
  495.3 4.8 multiply_convert_fusion.1
  504.4 8.9 %copy.94 = bf16[2048,1,128]{2,1,0:T(2,128)(2,1)} copy(bf16[2048,1,128]{2,0,1:T(8,128)(2,1)S(1)} %bitcast.256) | data formatting | bytes 1048576 | tf_op jit(solution)/shard_map/stack;reshape | solution.py:125
  523.4 6.0 pad_maximum_fusion.1
  529.4 31.4 %all-to-all-done.2 = bf16[2048,3,128]{2,1,0:T(4,128)(2,1)S(1)} async-done(((bf16[2048,3,128]{2,1,0:T(4,128)(2,1)}), bf16[2048,3,128]{2,1,0:T(4,128)(2,1)S(1)}, u32[]{:S(2)}, u32[]{:S(2)}) %all-to-all-start.2) | async-done | bytes 1572896 | tf_op jit(solution)/shard_map/all_to_all | solution.py:127
  560.8 8.9 %all-to-all-start.5 = ((bf16[2048,3,128]{2,1,0:T(4,128)(2,1)}), bf16[2048,3,128]{2,1,0:T(4,128)(2,1)}, u32[]{:S(2)}, u32[]{:S(2)}) async-start(bf16[2048,3,128]{2,1,0:T(4,128)(2,1)} %pad_maximum_fusion.1), calls=%async_computation.5 | async-start | bytes 4194304 | tf_op jit(solution)/shard_map/all_to_all | solution.py:127
  569.7 226.8 %reduce-scatter.3.cloned.1.call-done = f32[128,1536]{1,0:T(8,128)} async-done(((f32[2048,1536]{1,0:T(8,128)}), f32[128,1536]{1,0:T(8,128)}) %reduce-scatter.3.cloned.1.call-update) | async-done | bytes 786448 | tf_op jit(solution)/shard_map/reduce_scatter | solution.py:133
  809.6 66.0 %reduce-scatter.5.cloned.1.call-done = f32[8,1536]{1,0:T(8,128)} async-done(((f32[128,1536]{1,0:T(8,128)}), f32[8,1536]{1,0:T(8,128)}) %reduce-scatter.5.cloned.1.call-update) | async-done | bytes 49168 | tf_op jit(solution)/shard_map/reduce_scatter | solution.py:141
  (163 shorter events, 166.9 us)
Async XLA Ops:
  7.2 222.3 %all-gather.2.cloned.1.call-start = ((), (), s32[]{:S(2)}) async-start(), calls=%async_computation.10 | async-start | bytes 6684672 | tf_op jit(solution)/shard_map/all_gather | solution.py:96
  37.1 75.3 %all-to-all-start = ((bf16[128,3,2048]{0,1,2:T(4,128)(2,1)}), bf16[128,3,2048]{0,1,2:T(4,128)(2,1)S(1)}, u32[]{:S(2)}, u32[]{:S(2)}) async-start(bf16[128,3,2048]{0,1,2:T(4,128)(2,1)} %bitcast.246), calls=%async_computation | async-start | bytes 4194304 | tf_op jit(solution)/shard_map/all_to_all | solution.py:103
  44.9 80.7 %copy-start.9 = (bf16[2,128,1536]{2,1,0:T(8,128)(2,1)S(1)}, bf16[2,128,1536]{2,1,0:T(8,128)(2,1)}, u32[]{:S(2)}) copy-start(bf16[2,128,1536]{2,1,0:T(8,128)(2,1)} %param.9) | copy-start | bytes 2359300
  49.2 77.8 %copy-start.11 = (s32[1,16]{1,0:T(1,128)S(1)}, s32[1,16]{1,0:T(1,128)}, u32[]{:S(2)}) copy-start(s32[1,16]{1,0:T(1,128)} %param.13) | copy-start | bytes 196
  112.4 12.6 %copy-start.1 = (bf16[128,3,2048]{0,1,2:T(4,128)(2,1)}, bf16[128,3,2048]{0,1,2:T(4,128)(2,1)S(1)}, u32[]{:S(2)}) copy-start(bf16[128,3,2048]{0,1,2:T(4,128)(2,1)S(1)} %all-to-all-done) | copy-start | bytes 4718596
  112.4 140.0 %all-to-all-start.3 = ((bf16[128,3,2048]{0,1,2:T(4,128)(2,1)}), bf16[128,3,2048]{0,1,2:T(4,128)(2,1)}, u32[]{:S(2)}, u32[]{:S(2)}) async-start(bf16[128,3,2048]{0,1,2:T(4,128)(2,1)} %bitcast.16), calls=%async_computation.3 | async-start | bytes 4194304 | tf_op jit(solution)/shard_map/all_to_all | solution.py:103
  132.4 101.7 %copy-start.7 = (bf16[1,128,1536]{2,1,0:T(8,128)(2,1)}, bf16[1,128,1536]{2,1,0:T(8,128)(2,1)S(1)}, u32[]{:S(2)}) copy-start(bf16[1,128,1536]{2,1,0:T(8,128)(2,1)S(1)} %get-tuple-element.183) | copy-start | bytes 1179652
  132.4 101.7 %copy-start.8 = (bf16[1,128,1536]{2,1,0:T(8,128)(2,1)}, bf16[1,128,1536]{2,1,0:T(8,128)(2,1)S(1)}, u32[]{:S(2)}) copy-start(bf16[1,128,1536]{2,1,0:T(8,128)(2,1)S(1)} %get-tuple-element.184) | copy-start | bytes 1179652
  252.4 55.9 %all-to-all-start.1 = ((bf16[16,2,8192]{2,1,0:T(2,128)(2,1)}), bf16[16,2,8192]{2,1,0:T(2,128)(2,1)}, u32[]{:S(2)}, u32[]{:S(2)}) async-start(bf16[16,2,8192]{2,1,0:T(2,128)(2,1)} %reshape.96), calls=%async_computation.1 | async-start | bytes 1048576 | tf_op jit(solution)/shard_map/all_to_all | solution.py:104
  282.6 6.8 copy-start.5
  308.3 117.5 %all-to-all-start.4 = ((bf16[16,2,8192]{2,1,0:T(2,128)(2,1)}), bf16[16,2,8192]{2,1,0:T(2,128)(2,1)}, u32[]{:S(2)}, u32[]{:S(2)}) async-start(bf16[16,2,8192]{2,1,0:T(2,128)(2,1)} %reshape.94), calls=%async_computation.4 | async-start | bytes 1048576 | tf_op jit(solution)/shard_map/all_to_all | solution.py:104
  333.3 4.8 copy-start.2
  333.3 7.2 slice-start
  338.1 2.5 slice-start.1
  353.6 4.8 copy-start.2
  353.6 7.2 slice-start
  358.4 2.4 slice-start.1
  373.8 4.8 copy-start.2
  373.8 7.2 slice-start
  378.6 2.5 slice-start.1
  394.0 4.8 copy-start.2
  394.0 7.2 slice-start
  398.8 2.4 slice-start.1
  425.8 26.2 %all-to-all-start.6 = ((bf16[16,2,8192]{2,1,0:T(2,128)(2,1)}), bf16[16,2,8192]{2,1,0:T(2,128)(2,1)}, u32[]{:S(2)}, u32[]{:S(2)}) async-start(bf16[16,2,8192]{2,1,0:T(2,128)(2,1)} %reshape.100), calls=%async_computation.6 | async-start | bytes 1048576 | tf_op jit(solution)/shard_map/all_to_all | solution.py:128
  452.0 22.6 %all-to-all-start.7 = ((bf16[16,2,8192]{2,1,0:T(2,128)(2,1)}), bf16[16,2,8192]{2,1,0:T(2,128)(2,1)}, u32[]{:S(2)}, u32[]{:S(2)}) async-start(bf16[16,2,8192]{2,1,0:T(2,128)(2,1)} %reshape.98), calls=%async_computation.7 | async-start | bytes 1048576 | tf_op jit(solution)/shard_map/all_to_all | solution.py:128
  460.1 336.5 %reduce-scatter.3.cloned.1.call-start = ((), (), s32[]{:S(2)}) async-start(), calls=%async_computation.11 | async-start | bytes 13369344 | tf_op jit(solution)/shard_map/reduce_scatter | solution.py:133
  488.8 6.5 copy-start.4
  491.4 69.4 %all-to-all-start.2 = ((bf16[2048,3,128]{2,1,0:T(4,128)(2,1)}), bf16[2048,3,128]{2,1,0:T(4,128)(2,1)S(1)}, u32[]{:S(2)}, u32[]{:S(2)}) async-start(bf16[2048,3,128]{2,1,0:T(4,128)(2,1)} %copy.84), calls=%async_computation.2 | async-start | bytes 4194304 | tf_op jit(solution)/shard_map/all_to_all | solution.py:127
  495.3 6.8 copy-start.3
  502.1 11.3 %copy-start.6 = (bf16[4,128,2,64]{1,3,2,0:T(8,128)(2,1)S(1)}, bf16[4,128,2,64]{1,3,2,0:T(8,128)(2,1)}, u32[]{:S(2)}) copy-start(bf16[4,128,2,64]{1,3,2,0:T(8,128)(2,1)} %copy-done.5) | copy-start | bytes 393220
  560.8 239.8 %all-to-all-start.5 = ((bf16[2048,3,128]{2,1,0:T(4,128)(2,1)}), bf16[2048,3,128]{2,1,0:T(4,128)(2,1)}, u32[]{:S(2)}, u32[]{:S(2)}) async-start(bf16[2048,3,128]{2,1,0:T(4,128)(2,1)} %pad_maximum_fusion.1), calls=%async_computation.5 | async-start | bytes 4194304 | tf_op jit(solution)/shard_map/all_to_all | solution.py:127
  569.7 306.0 %reduce-scatter.5.cloned.1.call-start = ((), (), s32[]{:S(2)}) async-start(), calls=%async_computation.12 | async-start | bytes 835584 | tf_op jit(solution)/shard_map/reduce_scatter | solution.py:141
  (2 other events, 3.0 us)
Sparse Core Ops, SparseCore 0:
  31.2 198.2 all-gather.1
  486.8 309.7 reduce-scatter.2
  801.2 74.4 reduce-scatter.4
where the time goes:
time: 892 us; the launch traced here: 882 us
  waiting for transfers between devices  486 us (54%)
  local copies, waits for them, and re-layouts  115 us (13%)
  matrix products  93.8 us (11%)
  other arithmetic  79.1 us (9%)
  starting transfers between devices  68.9 us (8%)
  blocking collectives  23.9 us (3%)
  between operations  15.6 us (2%)
    reduce_scatter x1, waiting for transfers between devices, per_device(): lax.psum_scatter(jnp.einsum('vpt,vpg->tg', output_every, residual_gradien...  227 us
    all_gather x1, waiting for transfers between devices, per_device(): lax.all_gather(weight_group, 'seq', axis=0, tiled=True)  89 us
    reduce_scatter x1, waiting for transfers between devices, per_device(): lax.psum_scatter(group_part, 'dp', scatter_dimension=0, tiled=True)  66 us
    all_to_all x2, waiting for transfers between devices, per_device(): lax.all_to_all(qkv[step], 'seq', split_axis=2, concat_axis=0, tiled=True)  63.2 us
    unnamed x41, local copies, waits for them, and re-layouts  36.9 us
    sub x5, matrix products, one_block(): expo = jnp.exp(scores - top)  33.3 us
    all_to_all x2, waiting for transfers between devices, per_device(): lax.all_to_all(grads, 'seq', split_axis=0, concat_axis=2, tiled=True)  31.4 us
    unnamed x4, other arithmetic  25.8 us
  transfers between devices with their start and end apart: 11, of which 6 were waited for; matrix products, arithmetic and copies ran while one was open for 30% of the time, Pallas kernels for 0%

commit v1 on v0

v1 whole, which is shorter than its diff:
```python
import functools
import jax
import jax.numpy as jnp
from jax import lax
from jax.experimental import pallas as pl
from jax.experimental.pallas import tpu as pltpu
from jax.sharding import Mesh
from jax.sharding import PartitionSpec as P

HEAD_DIM = 64
FT = 128
KC = 256


def attn_kernel(rows_ref, x_ref, d_ref, o_ref, g_ref, dk_ref, dv_ref, kt_ref, vt_ref, s_ref, e_ref, *, frames, picked, scale):
    step = pl.program_id(0)
    length = frames * FT
    chunks = length // KC
    per = KC // FT
    width = 2 * HEAD_DIM
    block = d_ref.shape[0]

    @pl.when(step == 0)
    def _():
        dk_ref[...] = jnp.zeros_like(dk_ref)
        dv_ref[...] = jnp.zeros_like(dv_ref)
        for f in range(frames):
            kt_ref[:, f * FT:(f + 1) * FT] = x_ref[f, 1].T
            vt_ref[:, f * FT:(f + 1) * FT] = x_ref[f, 2].T
            if picked < frames:
                g_ref[f, 0] = jnp.zeros((FT, width), jnp.bfloat16)

    nb = block // FT
    own = [rows_ref[step * nb + j] for j in range(nb)]
    q = jnp.concatenate([x_ref[own[j], 0] for j in range(nb)], axis=0) * jnp.bfloat16(scale)
    do = d_ref[...]
    q_t = q.T
    do_t = do.T.astype(jnp.float32)
    lane = lax.broadcasted_iota(jnp.int32, (block, width), 1)
    sub = lax.broadcasted_iota(jnp.int32, (width, block), 0)
    zero_q = jnp.zeros_like(q)
    zero_t = jnp.zeros_like(q_t)
    f32 = jnp.float32

    def keys(which, c):
        return x_ref[c * per:(c + 1) * per, which].reshape(KC, width)

    deltas, do_scaled, outs = [], [], []
    for h in range(2):
        lo, hi = h * HEAD_DIM, (h + 1) * HEAD_DIM
        q_th = jnp.where((sub >= lo) & (sub < hi), q_t, zero_t)
        top = None
        for c in range(chunks):
            s = jnp.dot(keys(1, c), q_th, preferred_element_type=f32)
            s_ref[h, c * KC:(c + 1) * KC, :] = s
            part = jnp.max(s.reshape(KC // 8, 8, block), axis=0)
            top = part if top is None else jnp.maximum(top, part)
        top = jnp.max(top, axis=0, keepdims=True)
        total = jnp.zeros((8, block), f32)
        out_t = jnp.zeros((HEAD_DIM, block), f32)
        for c in range(chunks):
            e = jnp.exp(s_ref[h, c * KC:(c + 1) * KC, :] - top)
            total = total + jnp.sum(e.reshape(KC // 8, 8, block), axis=0)
            eb = e.astype(jnp.bfloat16)
            e_ref[h, c * KC:(c + 1) * KC, :] = eb
            out_t = out_t + jnp.dot(vt_ref[lo:hi, c * KC:(c + 1) * KC], eb, preferred_element_type=f32)
        inv = 1.0 / jnp.sum(total, axis=0, keepdims=True)
        out_b = (out_t * inv).astype(jnp.bfloat16)
        outs.append(out_b)
        scaled = (do_t[lo:hi] * inv).astype(jnp.bfloat16)
        do_scaled.append(scaled)
        deltas.append(jnp.sum(scaled.astype(f32) * out_b.astype(f32), axis=0, keepdims=True))
    o_ref[...] = jnp.concatenate(outs, axis=0).T
    ds_t = jnp.concatenate(do_scaled, axis=0)
    ds_row = ds_t.T
    dq_t = [jnp.zeros((HEAD_DIM, block), f32) for _ in range(2)]
    d_th = [jnp.where((sub >= h * HEAD_DIM) & (sub < (h + 1) * HEAD_DIM), ds_t, zero_t) for h in range(2)]
    d_row = [jnp.where((lane >= h * HEAD_DIM) & (lane < (h + 1) * HEAD_DIM), ds_row, zero_q) for h in range(2)]
    q_row = [jnp.where((lane >= h * HEAD_DIM) & (lane < (h + 1) * HEAD_DIM), q, zero_q) for h in range(2)]
    for c in range(chunks):
        rows = slice(c * KC, (c + 1) * KC)
        dk, dv = dk_ref[rows, :], dv_ref[rows, :]
        for h in range(2):
            lo, hi = h * HEAD_DIM, (h + 1) * HEAD_DIM
            dp = jnp.dot(keys(2, c), d_th[h], preferred_element_type=f32)
            eb = e_ref[h, rows, :]
            grad = (eb.astype(f32) * (dp - deltas[h])).astype(jnp.bfloat16)
            dq_t[h] = dq_t[h] + jnp.dot(kt_ref[lo:hi, rows], grad, preferred_element_type=f32)
            dk = dk + jnp.dot(grad, q_row[h], preferred_element_type=f32)
            dv = dv + jnp.dot(eb, d_row[h], preferred_element_type=f32)
        dk_ref[rows, :] = dk
        dv_ref[rows, :] = dv
    dq = (jnp.concatenate(dq_t, axis=0) * scale).astype(jnp.bfloat16).T
    for j in range(nb):
        g_ref[own[j], 0] = dq[j * FT:(j + 1) * FT]

    @pl.when(step == pl.num_programs(0) - 1)
    def _():
        for f in range(frames):
            g_ref[f, 1] = dk_ref[f * FT:(f + 1) * FT, :].astype(jnp.bfloat16)
            g_ref[f, 2] = dv_ref[f * FT:(f + 1) * FT, :].astype(jnp.bfloat16)


def attend(rows, heads, grads, block=256):
    frames, _, _, width = heads.shape
    picked = rows.shape[0]
    length = frames * FT
    whole = lambda i, r: (0, 0, 0, 0)
    kernel = functools.partial(attn_kernel, frames=frames, picked=picked, scale=HEAD_DIM ** -0.5)
    return pl.pallas_call(
        kernel,
        grid_spec=pltpu.PrefetchScalarGridSpec(
            num_scalar_prefetch=1,
            grid=(picked * FT // block,),
            in_specs=[
                pl.BlockSpec(heads.shape, whole),
                pl.BlockSpec((block, width), lambda i, r: (i, 0)),
            ],
            out_specs=[
                pl.BlockSpec((block, width), lambda i, r: (i, 0)),
                pl.BlockSpec(heads.shape, whole),
            ],
            scratch_shapes=[
                pltpu.VMEM((length, width), jnp.float32),
                pltpu.VMEM((length, width), jnp.float32),
                pltpu.VMEM((width, length), jnp.bfloat16),
                pltpu.VMEM((width, length), jnp.bfloat16),
                pltpu.VMEM((2, length, block), jnp.float32),
                pltpu.VMEM((2, length, block), jnp.bfloat16),
            ],
        ),
        out_shape=[
            jax.ShapeDtypeStruct((picked * FT, width), jnp.bfloat16),
            jax.ShapeDtypeStruct(heads.shape, jnp.bfloat16),
        ],
        compiler_params=pltpu.CompilerParams(vmem_limit_bytes=48 * 1024 * 1024),
        name="attend",
    )(rows, heads, grads)


def swap(value):
    return lax.ppermute(value, ("co", "yl"), [(0, 0), (1, 2), (2, 1), (3, 3)])


def live_frames(flags, count):
    frames = flags.shape[0]
    index = jnp.arange(frames, dtype=jnp.int32)
    free = flags == 0
    before = jnp.sum((index[None, :] < index[:, None]) & free[None, :], axis=1)
    hit = free[None, :] & (before[None, :] == jnp.arange(count, dtype=jnp.int32)[:, None])
    return jnp.sum(jnp.where(hit, index[None, :], 0), axis=1).astype(jnp.int32)


def split_heads(qkv_step, groups):
    tokens, three, inner = qkv_step.shape
    return jnp.transpose(qkv_step.reshape(tokens, three, groups, inner // groups), (2, 1, 0, 3))


def join_heads(blocks):
    groups, three, tokens, width = blocks.shape
    return jnp.transpose(blocks, (2, 1, 0, 3)).reshape(tokens, three, groups * width)


def per_device(qkv, cotangent, out_weight, gate_table, timestep, plan):
    seq, group = ("z", "yl"), ("co", "z")
    frames = lax.axis_size(seq)
    half = frames // 2
    live_count = frames // 4
    tokens, dout = cotangent.shape[1:]
    piece = tokens // frames
    gate_now = lax.dynamic_index_in_dim(gate_table, timestep[0], 0, keepdims=False)
    gate_prev = lax.dynamic_index_in_dim(gate_table, timestep[0] - 1, 0, keepdims=False)
    flags = plan[0]
    reuse = lax.dynamic_index_in_dim(flags, lax.axis_index(seq), 0, keepdims=False).astype(jnp.float32)
    live = live_frames(flags, live_count)
    grads_in = cotangent.astype(jnp.float32)
    res_one = (gate_now * grads_in[0] + reuse * (gate_prev * grads_in[1])).astype(jnp.bfloat16)
    res_two = ((1.0 - reuse) * (gate_prev * grads_in[1])).astype(jnp.bfloat16)

    heads_one = lax.all_to_all(split_heads(qkv[0], frames), seq, 0, 0, tiled=True)
    chunks = lax.all_to_all(res_two.reshape(frames, piece, dout), seq, 0, 0, tiled=True)
    chunks = chunks[live].reshape(live_count * piece, dout)
    rows = jnp.concatenate([res_one, chunks], axis=0)
    residual = lax.all_gather(swap(rows), group, axis=0)
    heads_two = lax.all_to_all(split_heads(qkv[1], frames), seq, 0, 0, tiled=True)
    weight = lax.all_gather(swap(out_weight), ("yh", "x", "yl"), axis=0, tiled=True)

    grad_rows = jnp.einsum(
        "rte,ke->rtk", residual, weight, preferred_element_type=jnp.float32
    ).astype(jnp.bfloat16)
    grad_rows = swap(grad_rows)
    width = grad_rows.shape[2]
    grad_one = jnp.swapaxes(grad_rows[:, :tokens].reshape(2, half, tokens, width), 0, 1)
    grad_two = grad_rows[:, tokens:].reshape(2, half, live_count, piece, width)
    grad_two = jnp.transpose(grad_two, (2, 1, 0, 3, 4))

    out_one, back_one = attend(
        jnp.arange(frames, dtype=jnp.int32), heads_one, grad_one.reshape(frames * tokens, width)
    )
    grads_one = lax.all_to_all(back_one, seq, 0, 0, tiled=True)
    out_two, back_two = attend(live, heads_two, grad_two.reshape(live_count * tokens, width))
    grads_two = lax.all_to_all(back_two, seq, 0, 0, tiled=True)

    out_one = jnp.swapaxes(out_one.reshape(half, 2, tokens, width), 0, 1)
    out_two = jnp.transpose(out_two.reshape(live_count, half, 2, piece, width), (2, 1, 0, 3, 4))
    outputs = jnp.concatenate(
        [out_one.reshape(frames, tokens, width), out_two.reshape(frames, live_count * piece, width)],
        axis=1,
    )
    outputs = swap(outputs)
    partial = jnp.einsum("rtk,rte->ke", outputs, residual, preferred_element_type=jnp.float32)
    parts = lax.all_to_all(
        partial.reshape(frames, width // frames, dout), ("yh", "x", "yl"), 0, 0, tiled=True
    )
    weight_grad = swap(jnp.sum(parts, axis=0))
    return jnp.stack([join_heads(grads_one), join_heads(grads_two)]), weight_grad


def solution(mesh):
    whole = Mesh(mesh.devices.reshape(2, 4, 2, 8, 2), ("yh", "x", "co", "z", "yl"))
    dp, seq = ("yh", "x", "co"), ("z", "yl")
    placed = (
        P(None, dp + seq, None, None),
        P(None, dp + seq, None),
        P(seq + dp, None),
        P(),
        P(dp),
        P(dp, None),
    )
    return jax.shard_map(
        per_device,
        mesh=whole,
        in_specs=placed,
        out_specs=(P(None, dp + seq, None, None), P(seq + dp, None)),
        check_vma=False,
    )
```

time: 892 us -> 377 us (0.42)
  waiting for transfers between devices: 486 us -> 95.9 us
  blocking collectives: 23.9 us -> 131 us
  local copies, waits for them, and re-layouts: 115 us -> 19.6 us
  matrix products: 93.8 us -> 9.89 us
  other arithmetic: 79.1 us -> 7.2 us
  Pallas kernels: 0 us -> 59 us
  starting transfers between devices: 68.9 us -> 35.4 us
    reduce_scatter x2 -> x0, waiting for transfers between devices: 293 us -> none  [the longest x1 227 us: per_device(): lax.psum_scatter(jnp.einsum('vpt,vpg->tg', output_every, residual_gradien...]
    all_gather x1, waiting for transfers between devices: 89 us -> 0.01 us  [per_device(): residual = lax.all_gather(swap(rows), group, axis=0)]
    all_to_all x0 -> x2, blocking collectives: none -> 85.5 us  [the longest x1 43.2 us: per_device(): grads_two = lax.all_to_all(back_two, seq, 0, 0, tiled=True)]
    pallas_call x0 -> x2, Pallas kernels: none -> 59 us  [attend(): pl.pallas_call(kernel, grid_spec=pltpu.PrefetchScalarGridSpec(num_scalar_...]
    dot_general x27 -> x2, matrix products: 60.5 us -> 9.89 us  [the longest x1 5.43 us: per_device(): jnp.einsum('rte,ke->rtk', residual, weight, preferred_element_type=jnp.fl...]
    all_to_all x8 -> x4, starting transfers between devices: 68.8 us -> 31.5 us  [the longest x1 12.4 us: per_device(): lax.all_to_all(split_heads(qkv[1], frames), seq, 0, 0, tiled=True)]
    sub x5 -> x0, matrix products: 33.3 us -> none  [one_block(): expo = jnp.exp(scores - top)]
    another operation x19 -> x2, local copies, waits for them, and re-layouts: 32.9 us -> 3.27 us  [split_heads(): qkv_step.reshape(tokens, three, groups, inner // groups)]
  transfers between devices with their start and end apart: 11 -> 10, of which waited for: 6 -> 3; matrix products, arithmetic and copies ran while one was open for 30% -> 5% of each run, Pallas kernels for 0% -> 3%
where the time goes in v1:
time: 377 us; the launch traced here: 374 us
  blocking collectives  131 us (35%)
  waiting for transfers between devices  95.9 us (25%)
  Pallas kernels  59 us (16%)
  starting transfers between devices  35.4 us (9%)
  local copies, waits for them, and re-layouts  19.6 us (5%)
  between operations  15.7 us (4%)
  matrix products  9.89 us (3%)
  other arithmetic  7.2 us (2%)
    pallas_call x2, Pallas kernels, attend(): pl.pallas_call(kernel, grid_spec=pltpu.PrefetchScalarGridSpec(num_scalar_...  59 us
    all_to_all x1, waiting for transfers between devices, per_device(): lax.all_to_all(split_heads(qkv[1], frames), seq, 0, 0, tiled=True)  50.8 us
    all_gather x1, blocking collectives, per_device(): lax.all_gather(swap(out_weight), ('yh', 'x', 'yl'), axis=0, tiled=True)  45.4 us
    all_to_all x1, blocking collectives, per_device(): grads_two = lax.all_to_all(back_two, seq, 0, 0, tiled=True)  43.2 us
    all_to_all x1, blocking collectives, per_device(): lax.all_to_all(partial.reshape(frames, width // frames, dout), ('yh', 'x'...  42.3 us
    all_to_all x1, waiting for transfers between devices, per_device(): grads_one = lax.all_to_all(back_one, seq, 0, 0, tiled=True)  31.7 us
    all_to_all x1, waiting for transfers between devices, per_device(): lax.all_to_all(res_two.reshape(frames, piece, dout), seq, 0, 0, tiled=True)  13.4 us
    all_to_all x1, starting transfers between devices, per_device(): lax.all_to_all(split_heads(qkv[1], frames), seq, 0, 0, tiled=True)  12.4 us
  transfers between devices with their start and end apart: 10, of which 3 were waited for; matrix products, arithmetic and copies ran while one was open for 5% of the time, Pallas kernels for 3%

profile of v1, /device:TPU:2, one launch (start us, length us, event | category | flops | bytes accessed | tf_op | source)
XLA Modules:
  0.0 373.7 jit_solution(14570552386747380441)
XLA Ops:
  7.8 1.3 convert_element_type.22
  10.4 0.9 dynamic-slice_reduce_fusion.1
  11.4 0.8 fusion.4
  12.2 9.6 %all-to-all-start.1 = ((bf16[16,8,1536]{2,1,0:T(8,128)(2,1)}), bf16[16,8,1536]{2,1,0:T(8,128)(2,1)S(1)}, u32[]{:S(2)}, u32[]{:S(2)}) async-start(bf16[16,8,1536]{2,1,0:T(8,128)(2,1)} %fusion.4), calls=%async_computation.1 | async-start | bytes 786432 | tf_op jit(solution)/shard_map/all_to_all | solution.py:181
  22.1 0.8 fusion.2
  22.9 13.4 %all-to-all-done.1 = bf16[16,8,1536]{2,1,0:T(8,128)(2,1)S(1)} async-done(((bf16[16,8,1536]{2,1,0:T(8,128)(2,1)}), bf16[16,8,1536]{2,1,0:T(8,128)(2,1)S(1)}, u32[]{:S(2)}, u32[]{:S(2)}) %all-to-all-start.1) | async-done | bytes 393248 | tf_op jit(solution)/shard_map/all_to_all | solution.py:181
  37.6 0.8 copy-done.2
  38.4 3.3 fusion.10
  41.7 0.9 copy.35
  42.7 1.6 copy.28
  44.2 12.4 %all-to-all-start.3 = ((bf16[16,3,128,128]{3,2,1,0:T(8,128)(2,1)}), bf16[16,3,128,128]{3,2,1,0:T(8,128)(2,1)S(1)}, u32[]{:S(2)}, u32[]{:S(2)}) async-start(bf16[16,3,128,128]{3,2,1,0:T(8,128)(2,1)} %bitcast.19), calls=%async_computation.3 | async-start | bytes 3145728 | tf_op jit(solution)/shard_map/all_to_all | solution.py:185
  56.6 2.0 copy.34
  58.6 1.7 copy.24
  60.3 50.8 %all-to-all-done.3.x_ref = bf16[16,3,128,128]{3,2,1,0:T(8,128)(2,1)S(1)} async-done(((bf16[16,3,128,128]{3,2,1,0:T(8,128)(2,1)}), bf16[16,3,128,128]{3,2,1,0:T(8,128)(2,1)S(1)}, u32[]{:S(2)}, u32[]{:S(2)}) %all-to-all-start.3) | async-done | bytes 1572896 | tf_op jit(solution)/shard_map/all_to_all | solution.py:185
  111.1 5.8 %all-to-all-start = ((bf16[16,3,128,128]{3,2,1,0:T(8,128)(2,1)}), bf16[16,3,128,128]{3,2,1,0:T(8,128)(2,1)S(1)}, u32[]{:S(2)}, u32[]{:S(2)}) async-start(bf16[16,3,128,128]{3,2,1,0:T(8,128)(2,1)} %bitcast.75), calls=%async_computation | async-start | bytes 3145728 | tf_op jit(solution)/shard_map/all_to_all | solution.py:180
  117.7 45.4 %all_gather.11 = bf16[128,1536]{1,0:T(8,128)(2,1)S(1)} all-gather(bf16[8,1536]{1,0:T(8,128)(2,1)S(1)} %collective-permute-done.1), channel_id=1, replica_groups=mesh['yh'=2,'x'=4,'co'=2,'z'=8,'yl'=2] {'yh','x','yl'}, dimensions={0}, use_global_device_ids=true | all-gather | bytes 417792 | tf_op jit(solution)/shard_map/all_gather | solution.py:186
  163.1 5.4 %convolution_convert_fusion = bf16[16,160,128]{2,1,0:T(8,128)(2,1)S(1)} fusion(bf16[16,160,1536]{2,1,0:T(8,128)(2,1)} %bitcast.73, bf16[128,1536]{1,0:T(8,128)(2,1)S(1)} %all_gather.11), kind=kOutput, calls=%fused_computation.3 | convolution fusion | flops 1006960640 | bytes 8912896 | tf_op jit(solution)/shard_map/rte,ke->rtk/dot_general | solution.py:188
  168.5 0.9 collective-permute-start.2
  169.5 12.3 %attend.3 = (bf16[512,128]{1,0:T(8,128)(2,1)S(1)}, bf16[16,3,128,128]{3,2,1,0:T(8,128)(2,1)S(1)}) custom-call(s32[4]{0:T(128)S(1)} %select_reduce_fusion.rows_ref, bf16[16,3,128,128]{3,2,1,0:T(8,128)(2,1)S(1)} %all-to-all-done.3.x_ref, bf16[512,128]{1,0:T(8,128)(2,1)S(1)} %bitcast.70), custom_call_target="tpu_custom_call" | custom-call | tf_op jit(solution)/shard_map/attend/pallas_call | solution.py:110
  181.8 1.1 copy-done
  183.1 46.7 %attend.2 = (bf16[2048,128]{1,0:T(8,128)(2,1)S(1)}, bf16[16,3,128,128]{3,2,1,0:T(8,128)(2,1)}) custom-call(s32[16]{0:T(128)S(1)} %iota.15.rows_ref, bf16[16,3,128,128]{3,2,1,0:T(8,128)(2,1)S(1)} %all-to-all-done.x_ref, bf16[2048,128]{1,0:T(8,128)(2,1)S(1)} %bitcast.69), custom_call_target="tpu_custom_call" | custom-call | tf_op jit(solution)/shard_map/attend/pallas_call | solution.py:110
  229.9 0.9 collective-permute-start.3
  230.8 4.5 %convolution_bitcast_fusion = f32[16,8,1536]{2,1,0:T(8,128)S(1)} fusion(bf16[16,160,128]{2,1,0:T(8,128)(2,1)S(1)} %collective-permute-done.3, bf16[16,160,1536]{2,1,0:T(8,128)(2,1)} %bitcast.74), kind=kOutput, calls=%fused_computation.2 | convolution fusion | flops 1006632960 | bytes 9306112 | tf_op jit(solution)/shard_map/rtk,rte->ke/dot_general | solution.py:211
  235.3 42.3 %all_to_all.30 = f32[16,8,1536]{2,1,0:T(8,128)} all-to-all(f32[16,8,1536]{2,1,0:T(8,128)S(1)} %convolution_bitcast_fusion), channel_id=1, replica_groups=mesh['yh'=2,'x'=4,'co'=2,'z'=8,'yl'=2] {'yh','x','yl'}, dimensions={0} | all-to-all | bytes 1572864 | tf_op jit(solution)/shard_map/all_to_all | solution.py:212
  277.6 43.2 %all_to_all.31 = bf16[16,3,128,128]{3,2,1,0:T(8,128)(2,1)S(1)} all-to-all(bf16[16,3,128,128]{3,2,1,0:T(8,128)(2,1)S(1)} %copy-done.1), channel_id=1, replica_groups=mesh['yh'=2,'x'=4,'co'=2,'z'=8,'yl'=2] {'z','yl'}, dimensions={0} | all-to-all | bytes 3145728 | tf_op jit(solution)/shard_map/all_to_all | solution.py:202
  320.8 3.7 all-to-all-start.2
  324.6 1.2 reduce_sum.32
  326.4 1.6 copy.30
  328.0 31.7 %all-to-all-done.2 = bf16[16,3,128,128]{3,2,1,0:T(8,128)(2,1)S(1)} async-done(((bf16[16,3,128,128]{3,2,1,0:T(8,128)(2,1)}), bf16[16,3,128,128]{3,2,1,0:T(8,128)(2,1)S(1)}, u32[]{:S(2)}, u32[]{:S(2)}) %all-to-all-start.2) | async-done | bytes 1572896 | tf_op jit(solution)/shard_map/all_to_all | solution.py:200
  359.7 1.6 copy.26
  361.2 2.2 pad_maximum_fusion
  363.4 2.8 copy.33
  (37 shorter events, 4.4 us)
Async XLA Ops:
  7.2 2.0 copy-start.4
  12.2 24.1 %all-to-all-start.1 = ((bf16[16,8,1536]{2,1,0:T(8,128)(2,1)}), bf16[16,8,1536]{2,1,0:T(8,128)(2,1)S(1)}, u32[]{:S(2)}, u32[]{:S(2)}) async-start(bf16[16,8,1536]{2,1,0:T(8,128)(2,1)} %fusion.4), calls=%async_computation.1 | async-start | bytes 786432 | tf_op jit(solution)/shard_map/all_to_all | solution.py:181
  21.8 141.3 %all-gather.3.cloned.1.call-start = ((), (), s32[]{:S(2)}) async-start(), calls=%async_computation.6 | async-start | bytes 8355840 | tf_op jit(solution)/shard_map/all_gather | solution.py:184
  36.9 0.7 collective-permute-start
  37.6 0.8 copy-start.2
  44.2 66.9 %all-to-all-start.3 = ((bf16[16,3,128,128]{3,2,1,0:T(8,128)(2,1)}), bf16[16,3,128,128]{3,2,1,0:T(8,128)(2,1)S(1)}, u32[]{:S(2)}, u32[]{:S(2)}) async-start(bf16[16,3,128,128]{3,2,1,0:T(8,128)(2,1)} %bitcast.19), calls=%async_computation.3 | async-start | bytes 3145728 | tf_op jit(solution)/shard_map/all_to_all | solution.py:185
  111.1 5.9 %copy-start.3 = (bf16[8,1536]{1,0:T(8,128)(2,1)S(1)}, bf16[8,1536]{1,0:T(8,128)(2,1)}, u32[]{:S(2)}) copy-start(bf16[8,1536]{1,0:T(8,128)(2,1)} %param.8) | copy-start | bytes 73732
  111.1 71.9 %all-to-all-start = ((bf16[16,3,128,128]{3,2,1,0:T(8,128)(2,1)}), bf16[16,3,128,128]{3,2,1,0:T(8,128)(2,1)S(1)}, u32[]{:S(2)}, u32[]{:S(2)}) async-start(bf16[16,3,128,128]{3,2,1,0:T(8,128)(2,1)} %bitcast.75), calls=%async_computation | async-start | bytes 3145728 | tf_op jit(solution)/shard_map/all_to_all | solution.py:180
  117.0 0.7 collective-permute-start.1
  168.5 0.9 collective-permute-start.2
  181.8 1.1 copy-start
  229.9 0.9 collective-permute-start.3
  235.3 42.3 %copy-start.1 = (bf16[16,3,128,128]{3,2,1,0:T(8,128)(2,1)S(1)}, bf16[16,3,128,128]{3,2,1,0:T(8,128)(2,1)}, u32[]{:S(2)}) copy-start(bf16[16,3,128,128]{3,2,1,0:T(8,128)(2,1)} %copy-done) | copy-start | bytes 4718596
  320.8 38.8 %all-to-all-start.2 = ((bf16[16,3,128,128]{3,2,1,0:T(8,128)(2,1)}), bf16[16,3,128,128]{3,2,1,0:T(8,128)(2,1)S(1)}, u32[]{:S(2)}, u32[]{:S(2)}) async-start(bf16[16,3,128,128]{3,2,1,0:T(8,128)(2,1)} %get-tuple-element.6), calls=%async_computation.2 | async-start | bytes 3145728 | tf_op jit(solution)/shard_map/all_to_all | solution.py:200
  325.7 0.7 collective-permute-start.4
Sparse Core Ops, SparseCore 0:
  38.5 120.4 all-gather.2

commit v2 on v1

v2 whole, which is shorter than its diff:
```python
import functools

import jax
import jax.numpy as jnp
from jax import lax
from jax.experimental import pallas as pl
from jax.experimental.pallas import tpu as pltpu
from jax.sharding import Mesh
from jax.sharding import PartitionSpec as P

HEAD_DIM = 64
FT = 128
KC = 1024
BLOCK = 256
WIDTH = 2 * HEAD_DIM
MIB = 1024 * 1024
PARAMS = pltpu.CompilerParams(vmem_limit_bytes=16 * MIB)
ATTEND_PARAMS = pltpu.CompilerParams(vmem_limit_bytes=20 * MIB)
RESIDENT = pl.BlockSpec(memory_space=pltpu.VMEM)
SMALL = pl.CostEstimate(flops=1000, transcendentals=0, bytes_accessed=1000)
F32 = jnp.float32
LOW = jnp.bfloat16


def prepare_kernel(time_ref, flags_ref, pos_ref, qkv_ref, cot_ref, gate_ref, sent_ref, one_ref):
    frames = sent_ref.shape[0]
    tokens, dout = one_ref.shape
    now = gate_ref[pl.ds(time_ref[0], 1), :]
    prev = gate_ref[pl.ds(time_ref[0] - 1, 1), :]
    reuse = flags_ref[pos_ref[0]].astype(F32)
    second = prev * cot_ref[1].astype(F32)
    one_ref[...] = (now * cot_ref[0].astype(F32) + reuse * second).astype(LOW)
    second = (1.0 - reuse) * second
    size = tokens // frames
    for f in range(frames):
        for w in range(3):
            sent_ref[f, w * FT:(w + 1) * FT, :] = qkv_ref[0, w, :, f * WIDTH:(f + 1) * WIDTH]
        rows = second[f * size:(f + 1) * size]
        parts = [rows[:, j * WIDTH:(j + 1) * WIDTH] for j in range(dout // WIDTH)]
        sent_ref[f, 3 * FT:, :] = jnp.concatenate(parts, axis=0).astype(LOW)


def prepare(timestep, flags, position, qkv, cotangent, gates, frames):
    _, three, tokens, inner = qkv.shape
    dout = cotangent.shape[2]
    sent = (frames, three * tokens + tokens * dout // frames // WIDTH, WIDTH)
    return pl.pallas_call(
        prepare_kernel,
        grid_spec=pltpu.PrefetchScalarGridSpec(
            num_scalar_prefetch=3,
            grid=(1,),
            in_specs=[
                pl.BlockSpec((1, three, tokens, inner), lambda *_: (1, 0, 0, 0)),
                RESIDENT,
                RESIDENT,
            ],
            out_specs=[RESIDENT, RESIDENT],
        ),
        out_shape=[
            jax.ShapeDtypeStruct(sent, LOW),
            jax.ShapeDtypeStruct((tokens, dout), LOW),
        ],
        compiler_params=PARAMS,
        cost_estimate=SMALL,
        name="prepare",
    )(timestep, flags, position, qkv, cotangent, gates)


def call_on(kernel, operands, shapes, dtype, name):
    count = len(operands)

    def body(*refs):
        kernel(refs[:count], refs[count:])

    return pl.pallas_call(
        body,
        in_specs=[RESIDENT] * count,
        out_specs=[RESIDENT] * len(shapes),
        out_shape=[jax.ShapeDtypeStruct(shape, dtype) for shape in shapes],
        compiler_params=PARAMS,
        cost_estimate=SMALL,
        name=name,
    )(*operands)


def first_pieces(refs):
    first, f1, f2, f3, f4, b1, b2, b3, b4 = refs
    rows = first.shape[0]
    far = jnp.concatenate([f4[...], b4[...]], axis=0)
    return [first[...], f1[...], f2[:rows], f3[:rows], far, b3[:rows], b2[:rows], b1[...]]


def second_pieces(refs, rows):
    second, f2, f3, f4, f5, b2, b3, b4, b5 = refs
    far = jnp.concatenate([f5[...], b5[...]], axis=0)
    return [second[...], f2[rows:], f3[rows:], f4[...], far, b4[...], b3[rows:], b2[rows:]]


def project(weight, other, ring, pieces_of):
    def kernel(held, outs):
        rows = jnp.concatenate([held[0][...], held[1][...]], axis=0)
        for j, piece in enumerate(pieces_of(held[2:])):
            got = lax.dot_general(piece, rows, (((1,), (1,)), ((), ())), preferred_element_type=F32)
            got = got.astype(LOW)
            for k in range(2):
                outs[k][j] = got[:, k * WIDTH:(k + 1) * WIDTH]

    shape = (lax.axis_size("z"), ring[0].shape[0], WIDTH)
    return call_on(kernel, [weight, other, *ring], [shape] * 2, LOW, "project")


def outer(outputs, ring_one, ring_two):
    count = len(ring_one)

    def kernel(held, outs):
        one = first_pieces(held[4:4 + count])
        two = second_pieces(held[4 + count:], held[4].shape[0])
        rows = jnp.concatenate(one + two, axis=0)
        for k in range(2):
            left = [held[k][...].reshape(-1, WIDTH), held[2 + k][...].reshape(-1, WIDTH)]
            left = jnp.concatenate(left, axis=0).T
            outs[k][...] = jnp.dot(left, rows, preferred_element_type=F32)

    shape = (WIDTH, ring_one[0].shape[1])
    return call_on(kernel, [*outputs, *ring_one, *ring_two], [shape] * 2, F32, "outer")


def split_kernel(qkv_ref, sent_ref):
    for f in range(sent_ref.shape[0]):
        for w in range(3):
            sent_ref[f, w * FT:(w + 1) * FT, :] = qkv_ref[0, w, :, f * WIDTH:(f + 1) * WIDTH]


def split_heads(qkv, step, frames):
    _, three, tokens, inner = qkv.shape
    sent = (frames, three * tokens, WIDTH)
    return pl.pallas_call(
        split_kernel,
        grid=(1,),
        in_specs=[pl.BlockSpec((1, three, tokens, inner), lambda i: (step, 0, 0, 0))],
        out_specs=RESIDENT,
        out_shape=jax.ShapeDtypeStruct(sent, LOW),
        compiler_params=PARAMS,
        cost_estimate=SMALL,
        name="split_heads",
    )(qkv)


def join_kernel(back_ref, *refs):
    out_ref = refs[-1]
    for f in range(back_ref.shape[0]):
        for w in range(3):
            out_ref[0, w, :, f * WIDTH:(f + 1) * WIDTH] = back_ref[f, w * FT:(w + 1) * FT, :]


def join_heads(back, step, held=None):
    frames, rows, width = back.shape
    shape = (2, 3, rows // 3, frames * width)
    specs, operands, aliases = [RESIDENT], [back], {}
    if held is not None:
        specs.append(pl.BlockSpec(memory_space=pl.ANY))
        operands.append(held)
        aliases = {1: 0}
    return pl.pallas_call(
        join_kernel,
        grid=(1,),
        in_specs=specs,
        out_specs=pl.BlockSpec((1,) + shape[1:], lambda i: (step, 0, 0, 0)),
        out_shape=jax.ShapeDtypeStruct(shape, LOW),
        input_output_aliases=aliases,
        compiler_params=PARAMS,
        cost_estimate=SMALL,
        name="join_heads",
    )(*operands)


def live_rows(rows_ref, at, size, live, back):
    count = live * FT
    place, low = rows_ref[live], rows_ref[live + 1]
    row = lax.broadcasted_iota(jnp.int32, (size, count), 0) + at
    col = lax.broadcasted_iota(jnp.int32, (size, count), 1)
    straight, ringed = (col, row) if back else (row, col)
    part = lax.rem(ringed, 8)
    frame = lax.rem(lax.div(ringed, 8), live)
    turn_by = lax.rem(lax.div(ringed, 8 * live), 8)
    side = lax.div(ringed, 64 * live)
    eighth = lax.rem(turn_by + place, 8)
    side = side + low - 2 * side * low
    return (straight == frame * FT + eighth * 16 + side * 8 + part).astype(F32).astype(LOW)


def attend_kernel(
    rows_ref, x_ref, d_ref, f_ref, o_ref, p_ref, g_ref, dk_ref, dv_ref, kt_ref, vt_ref, s_ref, e_ref,
    all_ref, *, scale, by_frame
):
    step = pl.program_id(0)
    frames, width = x_ref.shape[0], x_ref.shape[2]
    chunks = frames * FT // KC
    per, nb = KC // FT, BLOCK // FT

    @pl.when(step == 0)
    def _():
        dk_ref[...] = jnp.zeros_like(dk_ref)
        dv_ref[...] = jnp.zeros_like(dv_ref)
        for f in range(frames):
            kt_ref[:, f * FT:(f + 1) * FT] = x_ref[f, FT:2 * FT].T
            vt_ref[:, f * FT:(f + 1) * FT] = x_ref[f, 2 * FT:3 * FT].T
            if not by_frame:
                g_ref[f, 0:FT] = jnp.zeros((FT, width), LOW)

    own = [rows_ref[step * nb + j] for j in range(nb)]
    q = jnp.concatenate([x_ref[own[j], 0:FT] for j in range(nb)], axis=0) * LOW(scale)
    if by_frame:
        do = jnp.concatenate([d_ref[0], f_ref[0]], axis=0)
    else:
        live = rows_ref.shape[0] - 2
        ringed = [r[...].reshape(-1, width) for r in (d_ref, f_ref)]
        pick = live_rows(rows_ref, step * BLOCK, BLOCK, live, False)
        do = jnp.dot(pick, jnp.concatenate(ringed, axis=0), preferred_element_type=F32).astype(LOW)
    q_t = q.T
    do_t = do.T.astype(F32)
    lane = lax.broadcasted_iota(jnp.int32, (BLOCK, width), 1)
    sub = lax.broadcasted_iota(jnp.int32, (width, BLOCK), 0)
    zero, zero_t = jnp.zeros_like(q), jnp.zeros_like(q_t)
    in_lanes = [(lane >= h * HEAD_DIM) & (lane < (h + 1) * HEAD_DIM) for h in range(2)]
    in_subs = [(sub >= h * HEAD_DIM) & (sub < (h + 1) * HEAD_DIM) for h in range(2)]

    def part_of(which, c):
        return x_ref[c * per:(c + 1) * per, which * FT:(which + 1) * FT].reshape(KC, width)

    def fold(value):
        return value.reshape(value.shape[0] // 8, 8, value.shape[1])

    deltas, scaled, outs = [], [], []
    for h in range(2):
        lo, hi = h * HEAD_DIM, (h + 1) * HEAD_DIM
        q_th = jnp.where(in_subs[h], q_t, zero_t)
        top = None
        for c in range(chunks):
            s = jnp.dot(part_of(1, c), q_th, preferred_element_type=F32)
            s_ref[h, c * KC:(c + 1) * KC, :] = s
            part = jnp.max(fold(s), axis=0)
            top = part if top is None else jnp.maximum(top, part)
        top = jnp.max(top, axis=0, keepdims=True)
        total = jnp.zeros((8, BLOCK), F32)
        out_t = jnp.zeros((HEAD_DIM, BLOCK), F32)
        for c in range(chunks):
            rows = slice(c * KC, (c + 1) * KC)
            e = jnp.exp(s_ref[h, rows, :] - top)
            total = total + jnp.sum(fold(e), axis=0)
            eb = e.astype(LOW)
            e_ref[h, rows, :] = eb
            out_t = out_t + jnp.dot(vt_ref[lo:hi, rows], eb, preferred_element_type=F32)
        inv = 1.0 / jnp.sum(total, axis=0, keepdims=True)
        out_b = (out_t * inv).astype(LOW)
        outs.append(out_b)
        part = (do_t[lo:hi] * inv).astype(LOW)
        scaled.append(part)
        deltas.append(jnp.sum(part.astype(F32) * out_b.astype(F32), axis=0, keepdims=True))
    out = jnp.concatenate(outs, axis=0).T
    if by_frame:
        o_ref[0] = out[0:FT]
        p_ref[0] = out[FT:]
    else:
        all_ref[pl.ds(pl.multiple_of(step * BLOCK, BLOCK), BLOCK), :] = out
    ds_t = jnp.concatenate(scaled, axis=0)
    ds_row = ds_t.T
    dq_t = [jnp.zeros((HEAD_DIM, BLOCK), F32) for _ in range(2)]
    d_th = [jnp.where(in_subs[h], ds_t, zero_t) for h in range(2)]
    d_row = [jnp.where(in_lanes[h], ds_row, zero) for h in range(2)]
    q_row = [jnp.where(in_lanes[h], q, zero) for h in range(2)]
    for c in range(chunks):
        rows = slice(c * KC, (c + 1) * KC)
        gs, es = [], []
        both = jnp.dot(part_of(2, c), jnp.concatenate(d_th, axis=1), preferred_element_type=F32)
        for h in range(2):
            lo, hi = h * HEAD_DIM, (h + 1) * HEAD_DIM
            dp = both[:, h * BLOCK:(h + 1) * BLOCK]
            eb = e_ref[h, rows, :]
            grad = (eb.astype(F32) * (dp - deltas[h])).astype(LOW)
            dq_t[h] = dq_t[h] + jnp.dot(kt_ref[lo:hi, rows], grad, preferred_element_type=F32)
            gs.append(grad)
            es.append(eb)
        dk = dk_ref[rows, :] + jnp.dot(jnp.concatenate(gs, axis=1), jnp.concatenate(q_row, axis=0), preferred_element_type=F32)
        dv = dv_ref[rows, :] + jnp.dot(jnp.concatenate(es, axis=1), jnp.concatenate(d_row, axis=0), preferred_element_type=F32)
        dk_ref[rows, :] = dk
        dv_ref[rows, :] = dv
    dq = (jnp.concatenate(dq_t, axis=0) * scale).astype(LOW).T
    for j in range(nb):
        g_ref[own[j], 0:FT] = dq[j * FT:(j + 1) * FT]

    @pl.when(step == pl.num_programs(0) - 1)
    def _():
        for f in range(frames):
            g_ref[f, FT:2 * FT] = dk_ref[f * FT:(f + 1) * FT, :].astype(LOW)
            g_ref[f, 2 * FT:3 * FT] = dv_ref[f * FT:(f + 1) * FT, :].astype(LOW)
        if not by_frame:
            half = live * FT // 2
            for k, ref in enumerate((o_ref, p_ref)):
                pick = live_rows(rows_ref, k * half, half, live, True)
                ringed = jnp.dot(pick, all_ref[...], preferred_element_type=F32).astype(LOW)
                ref[...] = ringed.reshape(ref.shape)


def attend(rows, heads, grads, live=0):
    frames, _, width = heads.shape
    length = frames * FT
    steps = (live or frames) * FT // BLOCK
    back = (frames, 3 * FT, width)
    outputs = grads[0].shape
    ring = outputs[0]
    if live:
        spec = RESIDENT
    else:
        spec = pl.BlockSpec(
            (1, FT, width), lambda i, r: (lax.rem(i + ring - r[frames], ring), 0, 0)
        )
    return pl.pallas_call(
        functools.partial(attend_kernel, scale=HEAD_DIM ** -0.5, by_frame=not live),
        grid_spec=pltpu.PrefetchScalarGridSpec(
            num_scalar_prefetch=1,
            grid=(steps,),
            in_specs=[RESIDENT, spec, spec],
            out_specs=[spec, spec, RESIDENT],
            scratch_shapes=[
                pltpu.VMEM((length, width), F32),
                pltpu.VMEM((length, width), F32),
                pltpu.VMEM((width, length), LOW),
                pltpu.VMEM((width, length), LOW),
                pltpu.VMEM((2, length, BLOCK), F32),
                pltpu.VMEM((2, length, BLOCK), LOW),
                pltpu.VMEM((max(live * FT, FT), width), LOW),
            ],
        ),
        out_shape=[jax.ShapeDtypeStruct(outputs, LOW)] * 2 + [jax.ShapeDtypeStruct(back, LOW)],
        compiler_params=ATTEND_PARAMS,
        name="attend",
    )(rows, heads, *grads)


def swap(value):
    return lax.ppermute(value, ("co", "yl"), [(0, 0), (1, 2), (2, 1), (3, 3)])


def turn(value, axis, by):
    size = lax.axis_size(axis)
    return lax.ppermute(value, axis, [(i, (i + by) % size) for i in range(size)])


def pass_kernel(*refs):
    del refs


def after(value, *earlier):
    anywhere = pl.BlockSpec(memory_space=pl.ANY)
    return pl.pallas_call(
        pass_kernel,
        in_specs=[anywhere] * (1 + len(earlier)),
        out_specs=anywhere,
        out_shape=jax.ShapeDtypeStruct(value.shape, value.dtype),
        input_output_aliases={0: 0},
        cost_estimate=SMALL,
        name="after",
    )(value, *earlier)


def live_frames(flags, count):
    frames = flags.shape[0]
    index = jnp.arange(frames, dtype=jnp.int32)
    free = flags == 0
    before = jnp.sum((index[None, :] < index[:, None]) & free[None, :], axis=1)
    hit = free[None, :] & (before[None, :] == jnp.arange(count, dtype=jnp.int32)[:, None])
    return jnp.sum(jnp.where(hit, index[None, :], 0), axis=1).astype(jnp.int32)


def pair(value, axis):
    other = turn(value, axis, 1)
    first = lax.axis_index(axis) == 0
    return jnp.concatenate([jnp.where(first, value, other), jnp.where(first, other, value)], axis=0)


def cross(value, k, back=False):
    pairs = [(co * 2 + yl, yl * 2 + (co ^ k)) for co in range(2) for yl in range(2)]
    return lax.ppermute(value, ("co", "yl"), [p[::-1] for p in pairs] if back else pairs)


def ring_gather(first, second):
    rows = first.shape[0]
    cut, more = rows // 2, second.shape[0] // 2

    def both_ways(sign):
        one = turn(first, "z", sign)
        two = turn(jnp.concatenate([one, second], axis=0), "z", sign)
        three = turn(two, "z", sign)
        four = turn(three[rows:], "z", sign)
        half, quarter = (three[cut:rows], four[more:]) if sign > 0 else (three[:cut], four[:more])
        return one, two, three, turn(half, "z", sign), four, turn(quarter, "z", sign)

    b1, b2, b3, b4, d4, d5 = both_ways(1)
    f1, f2, f3, f4, e4, e5 = both_ways(-1)
    return [first, f1, f2, f3, f4, b1, b2, b3, b4], [second, f2, f3, e4, e5, b2, b3, d4, d5]


def gather_pair(value, axis, bit):
    size = lax.axis_size(axis)
    other = lax.ppermute(value, axis, [(i, i ^ bit) for i in range(size)])
    first = lax.axis_index(axis) & bit == 0
    return jnp.concatenate([jnp.where(first, value, other), jnp.where(first, other, value)], axis=0)


def gather_rows(shard):
    return gather_pair(gather_pair(shard, "yl", 1), "yh", 1)


def gather_weight(part):
    value = gather_pair(gather_pair(part, "x", 1), "x", 2)
    value = value.reshape(4, 2, -1, part.shape[1])
    return jnp.swapaxes(value, 0, 1).reshape(-1, part.shape[1])


def scatter_sum(value, axis):
    size = lax.axis_size(axis)
    here = lax.axis_index(axis)
    total = lax.dynamic_index_in_dim(value, here, 0, keepdims=False)
    for d in range(1, size):
        part = lax.dynamic_index_in_dim(value, (here + d) % size, 0, keepdims=False)
        total = total + turn(part, axis, d)
    return total


def last_sum(value):
    here, low = lax.axis_index("yh"), lax.axis_index("yl")
    every = [(yh, co, yl) for yh in range(2) for co in range(2) for yl in range(2)]
    total = None
    for h in range(2):
        for k in range(2):
            part = lax.dynamic_index_in_dim(value, here ^ h, 0, keepdims=False)
            part = lax.dynamic_index_in_dim(part, low ^ k, 0, keepdims=False)
            moves = [
                (yh * 4 + co * 2 + yl, (yh ^ h) * 4 + (yl ^ k) * 2 + co) for yh, co, yl in every
            ]
            part = lax.ppermute(part, ("yh", "co", "yl"), moves)
            total = part if total is None else total + part
    return total


def per_device(qkv, cotangent, out_weight, gate_table, timestep, plan):
    seq = ("z", "yl")
    place = lax.axis_index("z").astype(jnp.int32)
    low = lax.axis_index("yl").astype(jnp.int32)
    frames = lax.axis_size(seq)
    tokens, dout = cotangent.shape[1:]
    live_count = frames // 4
    flags = plan[0]
    live = live_frames(flags, live_count)
    position = lax.axis_index(seq).astype(jnp.int32).reshape(1)
    qkv = jnp.transpose(qkv, (0, 2, 1, 3))

    sent_two, res_one = prepare(timestep, flags, position, qkv, cotangent, gate_table, frames)
    heads_two = lax.all_to_all(sent_two, seq, 0, 0, tiled=True)
    weight = gather_weight(gather_rows(swap(out_weight)))
    other = turn(weight, "co", 1)
    chunks = heads_two[:, 3 * tokens:][live].reshape(live_count, dout // WIDTH, -1, WIDTH)
    chunks = after(jnp.swapaxes(chunks, 1, 2).reshape(-1, dout), other)
    ring_one, ring_two = ring_gather(swap(res_one), swap(chunks))
    grads_low = project(weight, other, ring_two, lambda refs: second_pieces(refs, tokens))
    grads_low = [cross(grads_low[k], k) for k in range(2)]
    sent_one = after(split_heads(qkv, 0, frames), ring_one[4], ring_one[8], ring_two[4], ring_two[8])
    heads_one = lax.all_to_all(sent_one, seq, 0, 0, tiled=True)
    grads = project(weight, other, ring_one, first_pieces)
    grads = [cross(grads[k], k) for k in range(2)]

    rows_two = jnp.concatenate([live, place[None], low[None]])
    *out_two, back_two = attend(rows_two, heads_two, grads_low, live_count)
    grads_two = lax.all_to_all(after(back_two, heads_one, *grads), seq, 0, 0, tiled=True)
    out_two = [cross(out_two[k], k, True) for k in range(2)]

    every = jnp.arange(frames, dtype=jnp.int32)
    rows_one = jnp.concatenate([every ^ low, place[None], low[None]])
    *out_one, back_one = attend(rows_one, heads_one, grads)
    grads_one = lax.all_to_all(after(back_one, grads_two), seq, 0, 0, tiled=True)
    held = join_heads(grads_two, 1)
    out_one = [cross(out_one[k], k, True) for k in range(2)]
    out_two[0] = after(out_two[0], held)
    partial = outer([*out_one, *out_two], ring_one, ring_two)
    total = partial[0] + turn(partial[1], "co", 1)
    total = jnp.transpose(total.reshape(2, 4, 2, -1, dout), (1, 0, 2, 3, 4))
    weight_grad = last_sum(scatter_sum(total, "x"))
    result = join_heads(grads_one, 0, held)
    return jnp.transpose(result, (0, 2, 1, 3)), weight_grad


def solution(mesh):
    split = Mesh(mesh.devices.reshape(2, 4, 2, 8, 2), ("yh", "x", "co", "z", "yl"))
    dp, seq = ("yh", "x", "co"), ("z", "yl")
    placed = (
        P(None, dp + seq, None, None),
        P(None, dp + seq, None),
        P(seq + dp, None),
        P(),
        P(dp),
        P(dp, None),
    )
    return jax.shard_map(
        per_device,
        mesh=split,
        in_specs=placed,
        out_specs=(P(None, dp + seq, None, None), P(seq + dp, None)),
        check_vma=False,
    )
```

time: 377 us -> 303 us (0.80)
  the two profiles are of different devices: /device:TPU:2 before, /device:TPU:1 now
where the time goes in v2:
time: 303 us; the launch traced here: 298 us
  starting transfers between devices  117 us (39%)
  waiting for transfers between devices  83.6 us (28%)
  Pallas kernels  58.3 us (19%)
  local copies, waits for them, and re-layouts  33.8 us (11%)
    pallas_call x2, Pallas kernels, attend(): pl.pallas_call(functools.partial(attend_kernel, scale=HEAD_DIM ** (-0.5),...  45.5 us
    ppermute x17, waiting for transfers between devices, turn(): lax.ppermute(value, axis, [(i, (i + by) % size) for i in range(size)])  34.2 us
    unnamed x116, local copies, waits for them, and re-layouts  30.6 us
    ppermute x17, starting transfers between devices, turn(): lax.ppermute(value, axis, [(i, (i + by) % size) for i in range(size)])  24.5 us
    all_to_all x1, starting transfers between devices, per_device(): lax.all_to_all(after(back_two, heads_one, *grads), seq, 0, 0, tiled=True)  24.5 us
    all_to_all x1, waiting for transfers between devices, per_device(): heads_two = lax.all_to_all(sent_two, seq, 0, 0, tiled=True)  20.4 us
    ppermute x8, starting transfers between devices, cross(): lax.ppermute(value, ('co', 'yl'), [p[::-1] for p in pairs] if back else p...  17.3 us
    ppermute x3, starting transfers between devices, swap(): return lax.ppermute(value, ('co', 'yl'), [(0, 0), (1, 2), (2, 1), (3, 3)])  15.5 us
  transfers between devices with their start and end apart: 40, of which 16 were waited for; matrix products, arithmetic and copies ran while one was open for 2% of the time, Pallas kernels for 19%

profile of v2, /device:TPU:1, one launch (start us, length us, event | category | flops | bytes accessed | tf_op | source)
XLA Modules:
  0.0 297.7 jit_solution(8327593065606638119)
XLA Ops:
  0.6 4.6 %collective-permute-start.2 = (bf16[8,1536]{1,0:T(8,128)(2,1)}, bf16[8,1536]{1,0:T(8,128)(2,1)S(1)}, u32[]{:S(2)}, u32[]{:S(2)}) collective-permute-start(bf16[8,1536]{1,0:T(8,128)(2,1)} %param.8), channel_id=1, source_target_pairs={{0,0},{1,16},{16,1},{17,17},{2,2},{3,18},{18,3},{19,19},{4,4},{5,2... | collective-permute-start | bytes 73736 | tf_op jit(solution)/shard_map/ppermute | solution.py:342
  14.6 9.6 %all-to-all-start = ((bf16[16,480,128]{2,1,0:T(8,128)(2,1)}), bf16[16,480,128]{2,1,0:T(8,128)(2,1)S(1)}, u32[]{:S(2)}, u32[]{:S(2)}) async-start(bf16[16,480,128]{2,1,0:T(8,128)(2,1)} %copy-done.29), calls=%async_computation | async-start | bytes 3932160 | tf_op jit(solution)/shard_map/all_to_all | solution.py:460
  24.2 2.9 collective-permute-start.4
  27.1 3.4 %collective-permute-done.4 = bf16[16,1536]{1,0:T(8,128)(2,1)S(1)} collective-permute-done((bf16[16,1536]{1,0:T(8,128)(2,1)S(1)}, bf16[16,1536]{1,0:T(8,128)(2,1)S(1)}, u32[]{:S(2)}, u32[]{:S(2)}) %collective-permute-start.4) | collective-permute-done | bytes 49184 | tf_op jit(solution)/shard_map/ppermute | solution.py:406
  31.8 4.9 %collective-permute-start = (bf16[128,1536]{1,0:T(8,128)(2,1)S(1)}, bf16[128,1536]{1,0:T(8,128)(2,1)}, u32[]{:S(2)}, u32[]{:S(2)}) collective-permute-start(bf16[128,1536]{1,0:T(8,128)(2,1)S(1)} %get-tuple-element.16), channel_id=1, source_target_pairs={{0,0},{1,16},{16,1},{17,17},{2,2},{3,18},{18,3},{19,19},{4,4},{5,2... | collective-permute-start | bytes 1179656 | tf_op jit(solution)/shard_map/ppermute | solution.py:342
  36.7 2.5 collective-permute-start.6
  39.4 4.9 %collective-permute-done.6 = bf16[64,1536]{1,0:T(8,128)(2,1)S(1)} collective-permute-done((bf16[64,1536]{1,0:T(8,128)(2,1)S(1)}, bf16[64,1536]{1,0:T(8,128)(2,1)S(1)}, u32[]{:S(2)}, u32[]{:S(2)}) %collective-permute-start.6) | collective-permute-done | bytes 196640 | tf_op jit(solution)/shard_map/ppermute | solution.py:406
  48.8 20.4 %all-to-all-done.x_ref = bf16[16,480,128]{2,1,0:T(8,128)(2,1)S(1)} async-done(((bf16[16,480,128]{2,1,0:T(8,128)(2,1)}), bf16[16,480,128]{2,1,0:T(8,128)(2,1)S(1)}, u32[]{:S(2)}, u32[]{:S(2)}) %all-to-all-start) | async-done | bytes 1966112 | tf_op jit(solution)/shard_map/all_to_all | solution.py:460
  73.0 6.1 %collective-permute-start.8 = (bf16[32,1536]{1,0:T(8,128)(2,1)}, bf16[32,1536]{1,0:T(8,128)(2,1)S(1)}, u32[]{:S(2)}, u32[]{:S(2)}) collective-permute-start(bf16[32,1536]{1,0:T(8,128)(2,1)} %after.5), channel_id=1, source_target_pairs={{0,0},{1,16},{16,1},{17,17},{2,2},{3,18},{18,3},{19,19},{4,4},{5,2... | collective-permute-start | bytes 294920 | tf_op jit(solution)/shard_map/ppermute | solution.py:342
  81.8 2.7 collective-permute-start.9
  84.4 9.5 %collective-permute-done.13.refs_8_.refs_7_.refs_10_.refs_18_ = bf16[160,1536]{1,0:T(8,128)(2,1)S(1)} collective-permute-done((bf16[160,1536]{1,0:T(8,128)(2,1)S(1)}, bf16[160,1536]{1,0:T(8,128)(2,1)S(1)}, u32[]{:S(2)}, u32[]{:S(2)}) %collective-permute-start.13) | collective-permute-done | bytes 491552 | tf_op jit(solution)/shard_map/ppermute | solution.py:347
  94.0 2.9 collective-permute-start.10
  96.9 10.3 %collective-permute-done.14.refs_9_.refs_8_.refs_11_.refs_19_ = bf16[160,1536]{1,0:T(8,128)(2,1)S(1)} collective-permute-done((bf16[160,1536]{1,0:T(8,128)(2,1)S(1)}, bf16[160,1536]{1,0:T(8,128)(2,1)S(1)}, u32[]{:S(2)}, u32[]{:S(2)}) %collective-permute-start.14) | collective-permute-done | bytes 491552 | tf_op jit(solution)/shard_map/ppermute | solution.py:347
  107.4 3.2 %collective-permute-start.11 = (bf16[64,1536]{1,0:T(8,128)(2,1)S(1)}, bf16[64,1536]{1,0:T(8,128)(2,1)S(1)}, u32[]{:S(2)}, u32[]{:S(2)}) collective-permute-start(bf16[64,1536]{1,0:T(8,128)(2,1)S(1)} %slice.31), channel_id=1, source_target_pairs={{0,14},{2,0},{4,2},{6,4},{8,6},{10,8},{12,10},{14,12},{1,15},{3,1}... | collective-permute-start | bytes 589832 | tf_op jit(solution)/shard_map/ppermute | solution.py:347
  110.7 2.7 collective-permute-start.16
  113.4 3.9 %collective-permute-done.18.refs_9_.refs_20_ = bf16[32,1536]{1,0:T(8,128)(2,1)S(1)} collective-permute-done((bf16[32,1536]{1,0:T(8,128)(2,1)S(1)}, bf16[32,1536]{1,0:T(8,128)(2,1)S(1)}, u32[]{:S(2)}, u32[]{:S(2)}) %collective-permute-start.18) | collective-permute-done | bytes 98336 | tf_op jit(solution)/shard_map/ppermute | solution.py:347
  118.8 2.6 collective-permute-start.17
  124.3 4.8 %all-to-all-start.1 = ((bf16[16,384,128]{2,1,0:T(8,128)(2,1)}), bf16[16,384,128]{2,1,0:T(8,128)(2,1)S(1)}, u32[]{:S(2)}, u32[]{:S(2)}) async-start(bf16[16,384,128]{2,1,0:T(8,128)(2,1)} %after.6), calls=%async_computation.1 | async-start | bytes 3145728 | tf_op jit(solution)/shard_map/all_to_all | solution.py:469
  135.0 3.1 %project.2 = (bf16[8,128,128]{2,1,0:T(8,128)(2,1)S(1)}, bf16[8,128,128]{2,1,0:T(8,128)(2,1)S(1)}) custom-call(bf16[128,1536]{1,0:T(8,128)(2,1)S(1)} %bitcast.45, bf16[128,1536]{1,0:T(8,128)(2,1)S(1)} %copy-done.28, bf16[128,1536]{1,0:T(8,128)(2,1)} %collective-permute-done.refs_2_.refs_4_, bf16[128,1536]{1,0:T(8,128)(2,1)S(1)} %copy-done.23, ...), custom_call_target="tpu_custom_call" | custom-call | flops 1000 | bytes 1000 | tf_op jit(solution)/shard_map/project/pallas_call | solution.py:75
  138.1 5.6 %collective-permute-start.20 = (bf16[8,128,128]{2,1,0:T(8,128)(2,1)S(1)}, bf16[8,128,128]{2,1,0:T(8,128)(2,1)S(1)}, u32[]{:S(2)}, u32[]{:S(2)}) collective-permute-start(bf16[8,128,128]{2,1,0:T(8,128)(2,1)S(1)} %get-tuple-element.18), channel_id=1, source_target_pairs={{0,0},{1,16},{16,1},{17,17},{2,2},{3,18},{18,3},{19,19},{4,4},{5,2... | collective-permute-start | bytes 786440 | tf_op jit(solution)/shard_map/ppermute | solution.py:384
  147.9 8.3 %collective-permute-done.22.d_ref = bf16[8,32,128]{2,1,0:T(8,128)(2,1)S(1)} collective-permute-done((bf16[8,32,128]{2,1,0:T(8,128)(2,1)S(1)}, bf16[8,32,128]{2,1,0:T(8,128)(2,1)S(1)}, u32[]{:S(2)}, u32[]{:S(2)}) %collective-permute-start.22) | collective-permute-done | bytes 65568 | tf_op jit(solution)/shard_map/ppermute | solution.py:384
  157.5 10.3 %attend.3 = (bf16[8,32,128]{2,1,0:T(8,128)(2,1)}, bf16[8,32,128]{2,1,0:T(8,128)(2,1)}, bf16[16,384,128]{2,1,0:T(8,128)(2,1)S(1)}) custom-call(s32[6]{0:T(128)S(1)} %pad_add_fusion.1.rows_ref, bf16[16,480,128]{2,1,0:T(8,128)(2,1)S(1)} %copy-done.12, bf16[8,32,128]{2,1,0:T(8,128)(2,1)S(1)} %collective-permute-done.22.d_ref, ...), custom_call_target="tpu_custom_call" | custom-call | tf_op jit(solution)/shard_map/attend/pallas_call | solution.py:318
  170.9 24.5 %all-to-all-start.2 = ((bf16[16,384,128]{2,1,0:T(8,128)(2,1)}), bf16[16,384,128]{2,1,0:T(8,128)(2,1)S(1)}, u32[]{:S(2)}, u32[]{:S(2)}) async-start(bf16[16,384,128]{2,1,0:T(8,128)(2,1)} %after.7), calls=%async_computation.2 | async-start | bytes 3145728 | tf_op jit(solution)/shard_map/all_to_all | solution.py:475
  195.5 35.1 %attend.2 = (bf16[8,128,128]{2,1,0:T(8,128)(2,1)}, bf16[8,128,128]{2,1,0:T(8,128)(2,1)}, bf16[16,384,128]{2,1,0:T(8,128)(2,1)S(1)}) custom-call(s32[18]{0:T(128)S(1)} %pad_add_fusion.rows_ref, bf16[16,384,128]{2,1,0:T(8,128)(2,1)S(1)} %copy-done.1, bf16[8,128,128]{2,1,0:T(8,128)(2,1)S(1)} %copy-done.37, ...), custom_call_target="tpu_custom_call" | custom-call | tf_op jit(solution)/shard_map/attend/pallas_call | solution.py:318
  232.9 7.8 %all-to-all-start.3 = ((bf16[16,384,128]{2,1,0:T(8,128)(2,1)}), bf16[16,384,128]{2,1,0:T(8,128)(2,1)S(1)}, u32[]{:S(2)}, u32[]{:S(2)}) async-start(bf16[16,384,128]{2,1,0:T(8,128)(2,1)} %after.8), calls=%async_computation.3 | async-start | bytes 3145728 | tf_op jit(solution)/shard_map/all_to_all | solution.py:481
  240.7 5.7 %collective-permute-start.24 = (bf16[8,128,128]{2,1,0:T(8,128)(2,1)}, bf16[8,128,128]{2,1,0:T(8,128)(2,1)}, u32[]{:S(2)}, u32[]{:S(2)}) collective-permute-start(bf16[8,128,128]{2,1,0:T(8,128)(2,1)} %get-tuple-element.24), channel_id=1, source_target_pairs={{0,0},{16,1},{1,16},{17,17},{2,2},{18,3},{3,18},{19,19},{4,4},{20,... | collective-permute-start | bytes 786440 | tf_op jit(solution)/shard_map/ppermute | solution.py:384
  246.6 3.6 %collective-permute-start.26 = (bf16[8,32,128]{2,1,0:T(8,128)(2,1)}, bf16[8,32,128]{2,1,0:T(8,128)(2,1)}, u32[]{:S(2)}, u32[]{:S(2)}) collective-permute-start(bf16[8,32,128]{2,1,0:T(8,128)(2,1)} %get-tuple-element.26), channel_id=1, source_target_pairs={{0,0},{16,1},{1,16},{17,17},{2,2},{18,3},{3,18},{19,19},{4,4},{20,... | collective-permute-start | bytes 196616 | tf_op jit(solution)/shard_map/ppermute | solution.py:384
  251.8 3.5 %collective-permute-done.26.refs_0_ = bf16[8,32,128]{2,1,0:T(8,128)(2,1)} collective-permute-done((bf16[8,32,128]{2,1,0:T(8,128)(2,1)}, bf16[8,32,128]{2,1,0:T(8,128)(2,1)}, u32[]{:S(2)}, u32[]{:S(2)}) %collective-permute-start.26) | collective-permute-done | bytes 65568 | tf_op jit(solution)/shard_map/ppermute | solution.py:384
  263.5 3.3 %outer.1 = (f32[128,1536]{1,0:T(8,128)S(1)}, f32[128,1536]{1,0:T(8,128)}) custom-call(bf16[8,128,128]{2,1,0:T(8,128)(2,1)} %collective-permute-done.24.refs_0_, bf16[8,128,128]{2,1,0:T(8,128)(2,1)} %collective-permute-done.25.refs_1_, bf16[8,32,128]{2,1,0:T(8,128)(2,1)} %after.9.refs_2_, bf16[8,32,128]{2,1,0:T(8,128)(2,1)} %collective-permute-done.27.refs_3_, ...), custom_call_target="tpu_custom_call" | custom-call | flops 1000 | bytes 1000 | tf_op jit(solution)/shard_map/outer/pallas_call | solution.py:75
  276.8 3.1 %collective-permute-done.29 = f32[2,2,8,1536]{3,2,1,0:T(8,128)S(1)} collective-permute-done((f32[2,2,8,1536]{3,2,1,0:T(8,128)S(1)}, f32[2,2,8,1536]{3,2,1,0:T(8,128)S(1)}, u32[]{:S(2)}, u32[]{:S(2)}) %collective-permute-start.29) | collective-permute-done | bytes 196640 | tf_op jit(solution)/shard_map/ppermute | solution.py:347
  279.9 5.2 %collective-permute-done.30 = f32[2,2,8,1536]{3,2,1,0:T(8,128)S(1)} collective-permute-done((f32[2,2,8,1536]{3,2,1,0:T(8,128)S(1)}, f32[2,2,8,1536]{3,2,1,0:T(8,128)S(1)}, u32[]{:S(2)}, u32[]{:S(2)}) %collective-permute-start.30) | collective-permute-done | bytes 196640 | tf_op jit(solution)/shard_map/ppermute | solution.py:347
  286.6 2.7 collective-permute-start.35
  (209 shorter events, 71.6 us)
Async XLA Ops:
  0.6 6.3 %collective-permute-start.2 = (bf16[8,1536]{1,0:T(8,128)(2,1)}, bf16[8,1536]{1,0:T(8,128)(2,1)S(1)}, u32[]{:S(2)}, u32[]{:S(2)}) collective-permute-start(bf16[8,1536]{1,0:T(8,128)(2,1)} %param.8), channel_id=1, source_target_pairs={{0,0},{1,16},{16,1},{17,17},{2,2},{3,18},{18,3},{19,19},{4,4},{5,2... | collective-permute-start | bytes 73736 | tf_op jit(solution)/shard_map/ppermute | solution.py:342
  6.9 17.2 %collective-permute-start.3 = (bf16[8,1536]{1,0:T(8,128)(2,1)S(1)}, bf16[8,1536]{1,0:T(8,128)(2,1)S(1)}, u32[]{:S(2)}, u32[]{:S(2)}) collective-permute-start(bf16[8,1536]{1,0:T(8,128)(2,1)S(1)} %collective-permute-done.2), channel_id=1, source_target_pairs={{0,1},{1,0},{2,3},{3,2},{4,5},{5,4},{6,7},{7,6},{8,9},{9,8},{10,11... | collective-permute-start | bytes 73736 | tf_op jit(solution)/shard_map/ppermute | solution.py:406
  14.6 54.7 %all-to-all-start = ((bf16[16,480,128]{2,1,0:T(8,128)(2,1)}), bf16[16,480,128]{2,1,0:T(8,128)(2,1)S(1)}, u32[]{:S(2)}, u32[]{:S(2)}) async-start(bf16[16,480,128]{2,1,0:T(8,128)(2,1)} %copy-done.29), calls=%async_computation | async-start | bytes 3932160 | tf_op jit(solution)/shard_map/all_to_all | solution.py:460
  24.2 6.2 %collective-permute-start.4 = (bf16[16,1536]{1,0:T(8,128)(2,1)S(1)}, bf16[16,1536]{1,0:T(8,128)(2,1)S(1)}, u32[]{:S(2)}, u32[]{:S(2)}) collective-permute-start(bf16[16,1536]{1,0:T(8,128)(2,1)S(1)} %pad_maximum_fusion.5), channel_id=1, source_target_pairs={{0,128},{128,0},{1,129},{129,1},{2,130},{130,2},{3,131},{131,3},{4... | collective-permute-start | bytes 147464 | tf_op jit(solution)/shard_map/ppermute | solution.py:406
  30.5 6.2 %collective-permute-start.5 = (bf16[32,1536]{1,0:T(8,128)(2,1)S(1)}, bf16[32,1536]{1,0:T(8,128)(2,1)S(1)}, u32[]{:S(2)}, u32[]{:S(2)}) collective-permute-start(bf16[32,1536]{1,0:T(8,128)(2,1)S(1)} %pad_maximum_fusion.4), channel_id=1, source_target_pairs={{0,32},{32,0},{64,96},{96,64},{1,33},{33,1},{65,97},{97,65},{2,34}... | collective-permute-start | bytes 294920 | tf_op jit(solution)/shard_map/ppermute | solution.py:406
  31.8 14.2 %collective-permute-start = (bf16[128,1536]{1,0:T(8,128)(2,1)S(1)}, bf16[128,1536]{1,0:T(8,128)(2,1)}, u32[]{:S(2)}, u32[]{:S(2)}) collective-permute-start(bf16[128,1536]{1,0:T(8,128)(2,1)S(1)} %get-tuple-element.16), channel_id=1, source_target_pairs={{0,0},{1,16},{16,1},{17,17},{2,2},{3,18},{18,3},{19,19},{4,4},{5,2... | collective-permute-start | bytes 1179656 | tf_op jit(solution)/shard_map/ppermute | solution.py:342
  36.7 7.6 %collective-permute-start.6 = (bf16[64,1536]{1,0:T(8,128)(2,1)S(1)}, bf16[64,1536]{1,0:T(8,128)(2,1)S(1)}, u32[]{:S(2)}, u32[]{:S(2)}) collective-permute-start(bf16[64,1536]{1,0:T(8,128)(2,1)S(1)} %pad_maximum_fusion.3), channel_id=1, source_target_pairs={{0,64},{32,96},{64,0},{96,32},{1,65},{33,97},{65,1},{97,33},{2,66}... | collective-permute-start | bytes 589832 | tf_op jit(solution)/shard_map/ppermute | solution.py:406
  44.5 27.7 %collective-permute-start.7 = (bf16[128,1536]{1,0:T(8,128)(2,1)S(1)}, bf16[128,1536]{1,0:T(8,128)(2,1)S(1)}, u32[]{:S(2)}, u32[]{:S(2)}) collective-permute-start(bf16[128,1536]{1,0:T(8,128)(2,1)S(1)} %bitcast.44), channel_id=1, source_target_pairs={{0,16},{16,0},{1,17},{17,1},{2,18},{18,2},{3,19},{19,3},{4,20},{20... | collective-permute-start | bytes 1179656 | tf_op jit(solution)/shard_map/ppermute | solution.py:347
  46.0 33.1 %collective-permute-start.12 = (bf16[128,1536]{1,0:T(8,128)(2,1)}, bf16[128,1536]{1,0:T(8,128)(2,1)S(1)}, u32[]{:S(2)}, u32[]{:S(2)}) collective-permute-start(bf16[128,1536]{1,0:T(8,128)(2,1)} %collective-permute-done.refs_2_.refs_4_), channel_id=1, source_target_pairs={{0,2},{2,4},{4,6},{6,8},{8,10},{10,12},{12,14},{14,0},{1,3},{3,5},... | collective-permute-start | bytes 1179656 | tf_op jit(solution)/shard_map/ppermute | solution.py:347
  47.3 31.8 %collective-permute-start.1 = (bf16[128,1536]{1,0:T(8,128)(2,1)}, bf16[128,1536]{1,0:T(8,128)(2,1)S(1)}, u32[]{:S(2)}, u32[]{:S(2)}) collective-permute-start(bf16[128,1536]{1,0:T(8,128)(2,1)} %collective-permute-done.refs_2_.refs_4_), channel_id=1, source_target_pairs={{0,14},{2,0},{4,2},{6,4},{8,6},{10,8},{12,10},{14,12},{1,15},{3,1}... | collective-permute-start | bytes 1179656 | tf_op jit(solution)/shard_map/ppermute | solution.py:347
  73.0 8.6 %collective-permute-start.8 = (bf16[32,1536]{1,0:T(8,128)(2,1)}, bf16[32,1536]{1,0:T(8,128)(2,1)S(1)}, u32[]{:S(2)}, u32[]{:S(2)}) collective-permute-start(bf16[32,1536]{1,0:T(8,128)(2,1)} %after.5), channel_id=1, source_target_pairs={{0,0},{1,16},{16,1},{17,17},{2,2},{3,18},{18,3},{19,19},{4,4},{5,2... | collective-permute-start | bytes 294920 | tf_op jit(solution)/shard_map/ppermute | solution.py:342
  81.7 12.3 %collective-permute-start.13 = (bf16[160,1536]{1,0:T(8,128)(2,1)S(1)}, bf16[160,1536]{1,0:T(8,128)(2,1)S(1)}, u32[]{:S(2)}, u32[]{:S(2)}) collective-permute-start(bf16[160,1536]{1,0:T(8,128)(2,1)S(1)} %get-tuple-element.41), channel_id=1, source_target_pairs={{0,2},{2,4},{4,6},{6,8},{8,10},{10,12},{12,14},{14,0},{1,3},{3,5},... | collective-permute-start | bytes 1474568 | tf_op jit(solution)/shard_map/ppermute | solution.py:347
  81.8 12.2 %collective-permute-start.9 = (bf16[160,1536]{1,0:T(8,128)(2,1)S(1)}, bf16[160,1536]{1,0:T(8,128)(2,1)S(1)}, u32[]{:S(2)}, u32[]{:S(2)}) collective-permute-start(bf16[160,1536]{1,0:T(8,128)(2,1)S(1)} %get-tuple-element.42), channel_id=1, source_target_pairs={{0,14},{2,0},{4,2},{6,4},{8,6},{10,8},{12,10},{14,12},{1,15},{3,1}... | collective-permute-start | bytes 1474568 | tf_op jit(solution)/shard_map/ppermute | solution.py:347
  94.0 13.3 %collective-permute-start.14 = (bf16[160,1536]{1,0:T(8,128)(2,1)S(1)}, bf16[160,1536]{1,0:T(8,128)(2,1)S(1)}, u32[]{:S(2)}, u32[]{:S(2)}) collective-permute-start(bf16[160,1536]{1,0:T(8,128)(2,1)S(1)} %collective-permute-done.13.refs_8_.refs_7_.refs_10_.refs_18_), channel_id=1, source_target_pairs={{0,2},{2,4},{4,6},{6,8},{8,10},{10,12},{12,14},{14,0},{1,3},{3,5},... | collective-permute-start | bytes 1474568 | tf_op jit(solution)/shard_map/ppermute | solution.py:347
  94.0 13.4 %collective-permute-start.10 = (bf16[160,1536]{1,0:T(8,128)(2,1)S(1)}, bf16[160,1536]{1,0:T(8,128)(2,1)S(1)}, u32[]{:S(2)}, u32[]{:S(2)}) collective-permute-start(bf16[160,1536]{1,0:T(8,128)(2,1)S(1)} %collective-permute-done.9.refs_4_.refs_3_.refs_6_.refs_14_), channel_id=1, source_target_pairs={{0,14},{2,0},{4,2},{6,4},{8,6},{10,8},{12,10},{14,12},{1,15},{3,1}... | collective-permute-start | bytes 1474568 | tf_op jit(solution)/shard_map/ppermute | solution.py:347
  107.3 15.7 %collective-permute-start.15 = (bf16[64,1536]{1,0:T(8,128)(2,1)S(1)}, bf16[64,1536]{1,0:T(8,128)(2,1)S(1)}, u32[]{:S(2)}, u32[]{:S(2)}) collective-permute-start(bf16[64,1536]{1,0:T(8,128)(2,1)S(1)} %slice.32), channel_id=1, source_target_pairs={{0,2},{2,4},{4,6},{6,8},{8,10},{10,12},{12,14},{14,0},{1,3},{3,5},... | collective-permute-start | bytes 589832 | tf_op jit(solution)/shard_map/ppermute | solution.py:347
  107.4 15.6 %collective-permute-start.11 = (bf16[64,1536]{1,0:T(8,128)(2,1)S(1)}, bf16[64,1536]{1,0:T(8,128)(2,1)S(1)}, u32[]{:S(2)}, u32[]{:S(2)}) collective-permute-start(bf16[64,1536]{1,0:T(8,128)(2,1)S(1)} %slice.31), channel_id=1, source_target_pairs={{0,14},{2,0},{4,2},{6,4},{8,6},{10,8},{12,10},{14,12},{1,15},{3,1}... | collective-permute-start | bytes 589832 | tf_op jit(solution)/shard_map/ppermute | solution.py:347
  110.6 6.7 %collective-permute-start.18 = (bf16[32,1536]{1,0:T(8,128)(2,1)S(1)}, bf16[32,1536]{1,0:T(8,128)(2,1)S(1)}, u32[]{:S(2)}, u32[]{:S(2)}) collective-permute-start(bf16[32,1536]{1,0:T(8,128)(2,1)S(1)} %slice.35), channel_id=1, source_target_pairs={{0,2},{2,4},{4,6},{6,8},{8,10},{10,12},{12,14},{14,0},{1,3},{3,5},... | collective-permute-start | bytes 294920 | tf_op jit(solution)/shard_map/ppermute | solution.py:347
  110.7 7.5 %collective-permute-start.16 = (bf16[32,1536]{1,0:T(8,128)(2,1)S(1)}, bf16[32,1536]{1,0:T(8,128)(2,1)S(1)}, u32[]{:S(2)}, u32[]{:S(2)}) collective-permute-start(bf16[32,1536]{1,0:T(8,128)(2,1)S(1)} %slice.33), channel_id=1, source_target_pairs={{0,14},{2,0},{4,2},{6,4},{8,6},{10,8},{12,10},{14,12},{1,15},{3,1}... | collective-permute-start | bytes 294920 | tf_op jit(solution)/shard_map/ppermute | solution.py:347
  124.3 45.4 %all-to-all-start.1 = ((bf16[16,384,128]{2,1,0:T(8,128)(2,1)}), bf16[16,384,128]{2,1,0:T(8,128)(2,1)S(1)}, u32[]{:S(2)}, u32[]{:S(2)}) async-start(bf16[16,384,128]{2,1,0:T(8,128)(2,1)} %after.6), calls=%async_computation.1 | async-start | bytes 3145728 | tf_op jit(solution)/shard_map/all_to_all | solution.py:469
  138.1 30.9 %collective-permute-start.20 = (bf16[8,128,128]{2,1,0:T(8,128)(2,1)S(1)}, bf16[8,128,128]{2,1,0:T(8,128)(2,1)S(1)}, u32[]{:S(2)}, u32[]{:S(2)}) collective-permute-start(bf16[8,128,128]{2,1,0:T(8,128)(2,1)S(1)} %get-tuple-element.18), channel_id=1, source_target_pairs={{0,0},{1,16},{16,1},{17,17},{2,2},{3,18},{18,3},{19,19},{4,4},{5,2... | collective-permute-start | bytes 786440 | tf_op jit(solution)/shard_map/ppermute | solution.py:384
  143.8 26.0 %collective-permute-start.21 = (bf16[8,128,128]{2,1,0:T(8,128)(2,1)S(1)}, bf16[8,128,128]{2,1,0:T(8,128)(2,1)}, u32[]{:S(2)}, u32[]{:S(2)}) collective-permute-start(bf16[8,128,128]{2,1,0:T(8,128)(2,1)S(1)} %get-tuple-element.19), channel_id=1, source_target_pairs={{0,1},{1,17},{16,0},{17,16},{2,3},{3,19},{18,2},{19,18},{4,5},{5,2... | collective-permute-start | bytes 786440 | tf_op jit(solution)/shard_map/ppermute | solution.py:384
  145.8 10.4 %collective-permute-start.22 = (bf16[8,32,128]{2,1,0:T(8,128)(2,1)S(1)}, bf16[8,32,128]{2,1,0:T(8,128)(2,1)S(1)}, u32[]{:S(2)}, u32[]{:S(2)}) collective-permute-start(bf16[8,32,128]{2,1,0:T(8,128)(2,1)S(1)} %get-tuple-element.21), channel_id=1, source_target_pairs={{0,0},{1,16},{16,1},{17,17},{2,2},{3,18},{18,3},{19,19},{4,4},{5,2... | collective-permute-start | bytes 196616 | tf_op jit(solution)/shard_map/ppermute | solution.py:384
  147.8 9.7 %collective-permute-start.23 = (bf16[8,32,128]{2,1,0:T(8,128)(2,1)S(1)}, bf16[8,32,128]{2,1,0:T(8,128)(2,1)S(1)}, u32[]{:S(2)}, u32[]{:S(2)}) collective-permute-start(bf16[8,32,128]{2,1,0:T(8,128)(2,1)S(1)} %get-tuple-element.22), channel_id=1, source_target_pairs={{0,1},{1,17},{16,0},{17,16},{2,3},{3,19},{18,2},{19,18},{4,5},{5,2... | collective-permute-start | bytes 196616 | tf_op jit(solution)/shard_map/ppermute | solution.py:384
  170.9 60.9 %all-to-all-start.2 = ((bf16[16,384,128]{2,1,0:T(8,128)(2,1)}), bf16[16,384,128]{2,1,0:T(8,128)(2,1)S(1)}, u32[]{:S(2)}, u32[]{:S(2)}) async-start(bf16[16,384,128]{2,1,0:T(8,128)(2,1)} %after.7), calls=%async_computation.2 | async-start | bytes 3145728 | tf_op jit(solution)/shard_map/all_to_all | solution.py:475
  232.9 63.0 %all-to-all-start.3 = ((bf16[16,384,128]{2,1,0:T(8,128)(2,1)}), bf16[16,384,128]{2,1,0:T(8,128)(2,1)S(1)}, u32[]{:S(2)}, u32[]{:S(2)}) async-start(bf16[16,384,128]{2,1,0:T(8,128)(2,1)} %after.8), calls=%async_computation.3 | async-start | bytes 3145728 | tf_op jit(solution)/shard_map/all_to_all | solution.py:481
  240.7 14.6 %collective-permute-start.24 = (bf16[8,128,128]{2,1,0:T(8,128)(2,1)}, bf16[8,128,128]{2,1,0:T(8,128)(2,1)}, u32[]{:S(2)}, u32[]{:S(2)}) collective-permute-start(bf16[8,128,128]{2,1,0:T(8,128)(2,1)} %get-tuple-element.24), channel_id=1, source_target_pairs={{0,0},{16,1},{1,16},{17,17},{2,2},{18,3},{3,18},{19,19},{4,4},{20,... | collective-permute-start | bytes 786440 | tf_op jit(solution)/shard_map/ppermute | solution.py:384
  246.4 8.9 %collective-permute-start.25 = (bf16[8,128,128]{2,1,0:T(8,128)(2,1)}, bf16[8,128,128]{2,1,0:T(8,128)(2,1)}, u32[]{:S(2)}, u32[]{:S(2)}) collective-permute-start(bf16[8,128,128]{2,1,0:T(8,128)(2,1)} %get-tuple-element.25), channel_id=1, source_target_pairs={{1,0},{17,1},{0,16},{16,17},{3,2},{19,3},{2,18},{18,19},{5,4},{21,... | collective-permute-start | bytes 786440 | tf_op jit(solution)/shard_map/ppermute | solution.py:384
  246.6 8.8 %collective-permute-start.26 = (bf16[8,32,128]{2,1,0:T(8,128)(2,1)}, bf16[8,32,128]{2,1,0:T(8,128)(2,1)}, u32[]{:S(2)}, u32[]{:S(2)}) collective-permute-start(bf16[8,32,128]{2,1,0:T(8,128)(2,1)} %get-tuple-element.26), channel_id=1, source_target_pairs={{0,0},{16,1},{1,16},{17,17},{2,2},{18,3},{3,18},{19,19},{4,4},{20,... | collective-permute-start | bytes 196616 | tf_op jit(solution)/shard_map/ppermute | solution.py:384
  272.5 7.4 %collective-permute-start.29 = (f32[2,2,8,1536]{3,2,1,0:T(8,128)S(1)}, f32[2,2,8,1536]{3,2,1,0:T(8,128)S(1)}, u32[]{:S(2)}, u32[]{:S(2)}) collective-permute-start(f32[2,2,8,1536]{3,2,1,0:T(8,128)S(1)} %get-tuple-element.30), channel_id=1, source_target_pairs={{0,32},{32,64},{64,96},{96,0},{1,33},{33,65},{65,97},{97,1},{2,34}... | collective-permute-start | bytes 589832 | tf_op jit(solution)/shard_map/ppermute | solution.py:347
  275.3 9.8 %collective-permute-start.30 = (f32[2,2,8,1536]{3,2,1,0:T(8,128)S(1)}, f32[2,2,8,1536]{3,2,1,0:T(8,128)S(1)}, u32[]{:S(2)}, u32[]{:S(2)}) collective-permute-start(f32[2,2,8,1536]{3,2,1,0:T(8,128)S(1)} %get-tuple-element.32), channel_id=1, source_target_pairs={{0,64},{32,96},{64,0},{96,32},{1,65},{33,97},{65,1},{97,33},{2,66}... | collective-permute-start | bytes 589832 | tf_op jit(solution)/shard_map/ppermute | solution.py:347
  285.2 6.6 %collective-permute-start.33 = (f32[8,1536]{1,0:T(8,128)S(1)}, f32[8,1536]{1,0:T(8,128)S(1)}, u32[]{:S(2)}, u32[]{:S(2)}) collective-permute-start(f32[8,1536]{1,0:T(8,128)S(1)} %get-tuple-element.35), channel_id=1, source_target_pairs={{0,16},{1,0},{16,17},{17,1},{128,144},{129,128},{144,145},{145,129... | collective-permute-start | bytes 147464 | tf_op jit(solution)/shard_map/ppermute | solution.py:442
  (66 other events, 618.2 us)

commit v3 on v2

--- a/solution.py
+++ b/solution.py
@@ -97,6 +97,8 @@
 
 
 def project(weight, other, ring, pieces_of):
+    count, columns = ring[0].shape
+
     def kernel(held, outs):
         rows = jnp.concatenate([held[0][...], held[1][...]], axis=0)
         for j, piece in enumerate(pieces_of(held[2:])):
@@ -104,25 +106,25 @@
             got = got.astype(LOW)
             for k in range(2):
                 outs[k][j] = got[:, k * WIDTH:(k + 1) * WIDTH]
-
-    shape = (lax.axis_size("z"), ring[0].shape[0], WIDTH)
-    return call_on(kernel, [weight, other, *ring], [shape] * 2, LOW, "project")
-
-
-def outer(outputs, ring_one, ring_two):
-    count = len(ring_one)
-
+            outs[2][j * count:(j + 1) * count] = piece
+
+    size = lax.axis_size("z")
+    shapes = [(size, count, WIDTH)] * 2 + [(size * count, columns)]
+    return call_on(kernel, [weight, other, *ring], shapes, LOW, "project")
+
+
+def outer(outputs, rows_one, rows_two):
     def kernel(held, outs):
-        one = first_pieces(held[4:4 + count])
-        two = second_pieces(held[4 + count:], held[4].shape[0])
-        rows = jnp.concatenate(one + two, axis=0)
         for k in range(2):
-            left = [held[k][...].reshape(-1, WIDTH), held[2 + k][...].reshape(-1, WIDTH)]
-            left = jnp.concatenate(left, axis=0).T
-            outs[k][...] = jnp.dot(left, rows, preferred_element_type=F32)
-
-    shape = (WIDTH, ring_one[0].shape[1])
-    return call_on(kernel, [*outputs, *ring_one, *ring_two], [shape] * 2, F32, "outer")
+            total = None
+            for out, rows in ((held[k], held[4]), (held[2 + k], held[5])):
+                left = out[...].reshape(-1, WIDTH).T
+                part = jnp.dot(left, rows[...], preferred_element_type=F32)
+                total = part if total is None else total + part
+            outs[k][...] = total
+
+    shape = (WIDTH, rows_one.shape[1])
+    return call_on(kernel, [*outputs, rows_one, rows_two], [shape] * 2, F32, "outer")
 
 
 def split_kernel(qkv_ref, sent_ref):
@@ -461,18 +463,20 @@
     weight = gather_weight(gather_rows(swap(out_weight)))
     other = turn(weight, "co", 1)
     chunks = heads_two[:, 3 * tokens:][live].reshape(live_count, dout // WIDTH, -1, WIDTH)
-    chunks = after(jnp.swapaxes(chunks, 1, 2).reshape(-1, dout), other)
-    ring_one, ring_two = ring_gather(swap(res_one), swap(chunks))
-    grads_low = project(weight, other, ring_two, lambda refs: second_pieces(refs, tokens))
+    chunks = swap(jnp.swapaxes(chunks, 1, 2).reshape(-1, dout))
+    ring_one, ring_two = ring_gather(swap(res_one), after(chunks, other))
+    *grads_low, rows_low = project(
+        weight, other, ring_two, lambda refs: second_pieces(refs, tokens)
+    )
     grads_low = [cross(grads_low[k], k) for k in range(2)]
-    sent_one = after(split_heads(qkv, 0, frames), ring_one[4], ring_one[8], ring_two[4], ring_two[8])
+    sent_one = after(split_heads(qkv, 0, frames), ring_one[4], ring_one[8], *grads_low)
     heads_one = lax.all_to_all(sent_one, seq, 0, 0, tiled=True)
-    grads = project(weight, other, ring_one, first_pieces)
+    *grads, rows_high = project(weight, other, ring_one, first_pieces)
     grads = [cross(grads[k], k) for k in range(2)]
 
     rows_two = jnp.concatenate([live, place[None], low[None]])
     *out_two, back_two = attend(rows_two, heads_two, grads_low, live_count)
-    grads_two = lax.all_to_all(after(back_two, heads_one, *grads), seq, 0, 0, tiled=True)
+    grads_two = lax.all_to_all(after(back_two, *grads), seq, 0, 0, tiled=True)
     out_two = [cross(out_two[k], k, True) for k in range(2)]
 
     every = jnp.arange(frames, dtype=jnp.int32)
@@ -482,7 +486,7 @@
     held = join_heads(grads_two, 1)
     out_one = [cross(out_one[k], k, True) for k in range(2)]
     out_two[0] = after(out_two[0], held)
-    partial = outer([*out_one, *out_two], ring_one, ring_two)
+    partial = outer([*out_one, *out_two], rows_high, rows_low)
     total = partial[0] + turn(partial[1], "co", 1)
     total = jnp.transpose(total.reshape(2, 4, 2, -1, dout), (1, 0, 2, 3, 4))
     weight_grad = last_sum(scatter_sum(total, "x"))

time: 303 us -> 290 us (0.957)
  the two profiles are of different devices: /device:TPU:1 before, /device:TPU:2 now
where the time goes in v3:
time: 290 us; the launch traced here: 284 us
  starting transfers between devices  97.6 us (34%)
  waiting for transfers between devices  89.7 us (31%)
  Pallas kernels  58.2 us (20%)
  local copies, waits for them, and re-layouts  33.3 us (11%)
  other arithmetic  3.58 us (1%)
    pallas_call x2, Pallas kernels, attend(): pl.pallas_call(functools.partial(attend_kernel, scale=HEAD_DIM ** (-0.5),...  44.7 us
    ppermute x17, waiting for transfers between devices, turn(): lax.ppermute(value, axis, [(i, (i + by) % size) for i in range(size)])  38.7 us
    unnamed x96, local copies, waits for them, and re-layouts  30.1 us
    ppermute x17, starting transfers between devices, turn(): lax.ppermute(value, axis, [(i, (i + by) % size) for i in range(size)])  23.6 us
    all_to_all x1, waiting for transfers between devices, per_device(): heads_two = lax.all_to_all(sent_two, seq, 0, 0, tiled=True)  16.3 us
    all_to_all x1, starting transfers between devices, per_device(): grads_two = lax.all_to_all(after(back_two, *grads), seq, 0, 0, tiled=True)  15.6 us
    ppermute x4, waiting for transfers between devices, gather_pair(): other = lax.ppermute(value, axis, [(i, i ^ bit) for i in range(size)])  13.9 us
    ppermute x8, waiting for transfers between devices, cross(): lax.ppermute(value, ('co', 'yl'), [p[::-1] for p in pairs] if back else p...  12.4 us
  transfers between devices with their start and end apart: 40, of which 22 were waited for; matrix products, arithmetic and copies ran while one was open for 2% of the time, Pallas kernels for 20%

profile of v3, /device:TPU:2, one launch (start us, length us, event | category | flops | bytes accessed | tf_op | source)
XLA Modules:
  0.0 284.3 jit_solution(3687335653728367357)
XLA Ops:
  8.2 9.7 %all-to-all-start = ((bf16[16,480,128]{2,1,0:T(8,128)(2,1)}), bf16[16,480,128]{2,1,0:T(8,128)(2,1)S(1)}, u32[]{:S(2)}, u32[]{:S(2)}) async-start(bf16[16,480,128]{2,1,0:T(8,128)(2,1)} %copy-done.22), calls=%async_computation | async-start | bytes 3932160 | tf_op jit(solution)/shard_map/all_to_all | solution.py:462
  18.7 6.4 %collective-permute-start.4 = (bf16[8,1536]{1,0:T(8,128)(2,1)S(1)}, bf16[8,1536]{1,0:T(8,128)(2,1)S(1)}, u32[]{:S(2)}, u32[]{:S(2)}) collective-permute-start(bf16[8,1536]{1,0:T(8,128)(2,1)S(1)} %collective-permute-done.3), channel_id=1, source_target_pairs={{0,1},{1,0},{2,3},{3,2},{4,5},{5,4},{6,7},{7,6},{8,9},{9,8},{10,11... | collective-permute-start | bytes 73736 | tf_op jit(solution)/shard_map/ppermute | solution.py:408
  26.9 3.0 %collective-permute-start.5 = (bf16[16,1536]{1,0:T(8,128)(2,1)S(1)}, bf16[16,1536]{1,0:T(8,128)(2,1)S(1)}, u32[]{:S(2)}, u32[]{:S(2)}) collective-permute-start(bf16[16,1536]{1,0:T(8,128)(2,1)S(1)} %pad_maximum_fusion.5), channel_id=1, source_target_pairs={{0,128},{128,0},{1,129},{129,1},{2,130},{130,2},{3,131},{131,3},{4... | collective-permute-start | bytes 147464 | tf_op jit(solution)/shard_map/ppermute | solution.py:408
  33.2 4.9 %collective-permute-done.6 = bf16[32,1536]{1,0:T(8,128)(2,1)S(1)} collective-permute-done((bf16[32,1536]{1,0:T(8,128)(2,1)S(1)}, bf16[32,1536]{1,0:T(8,128)(2,1)S(1)}, u32[]{:S(2)}, u32[]{:S(2)}) %collective-permute-start.6) | collective-permute-done | bytes 98336 | tf_op jit(solution)/shard_map/ppermute | solution.py:408
  40.7 5.9 %collective-permute-done.7 = bf16[64,1536]{1,0:T(8,128)(2,1)S(1)} collective-permute-done((bf16[64,1536]{1,0:T(8,128)(2,1)S(1)}, bf16[64,1536]{1,0:T(8,128)(2,1)S(1)}, u32[]{:S(2)}, u32[]{:S(2)}) %collective-permute-start.7) | collective-permute-done | bytes 196640 | tf_op jit(solution)/shard_map/ppermute | solution.py:408
  46.8 2.8 collective-permute-start.1
  49.5 16.3 %all-to-all-done.x_ref = bf16[16,480,128]{2,1,0:T(8,128)(2,1)S(1)} async-done(((bf16[16,480,128]{2,1,0:T(8,128)(2,1)}), bf16[16,480,128]{2,1,0:T(8,128)(2,1)S(1)}, u32[]{:S(2)}, u32[]{:S(2)}) %all-to-all-start) | async-done | bytes 1966112 | tf_op jit(solution)/shard_map/all_to_all | solution.py:462
  75.2 10.9 %collective-permute-done.9.refs_3_.refs_4_ = bf16[160,1536]{1,0:T(8,128)(2,1)S(1)} collective-permute-done((bf16[160,1536]{1,0:T(8,128)(2,1)S(1)}, bf16[160,1536]{1,0:T(8,128)(2,1)S(1)}, u32[]{:S(2)}, u32[]{:S(2)}) %collective-permute-start.9) | collective-permute-done | bytes 491552 | tf_op jit(solution)/shard_map/ppermute | solution.py:349
  86.1 2.9 %collective-permute-start.10 = (bf16[160,1536]{1,0:T(8,128)(2,1)S(1)}, bf16[160,1536]{1,0:T(8,128)(2,1)S(1)}, u32[]{:S(2)}, u32[]{:S(2)}) collective-permute-start(bf16[160,1536]{1,0:T(8,128)(2,1)S(1)} %collective-permute-done.9.refs_3_.refs_4_), channel_id=1, source_target_pairs={{0,14},{2,0},{4,2},{6,4},{8,6},{10,8},{12,10},{14,12},{1,15},{3,1}... | collective-permute-start | bytes 1474568 | tf_op jit(solution)/shard_map/ppermute | solution.py:349
  89.3 11.0 %collective-permute-done.10.refs_4_.refs_5_ = bf16[160,1536]{1,0:T(8,128)(2,1)S(1)} collective-permute-done((bf16[160,1536]{1,0:T(8,128)(2,1)S(1)}, bf16[160,1536]{1,0:T(8,128)(2,1)S(1)}, u32[]{:S(2)}, u32[]{:S(2)}) %collective-permute-start.10) | collective-permute-done | bytes 491552 | tf_op jit(solution)/shard_map/ppermute | solution.py:349
  100.3 3.8 %collective-permute-start.16 = (bf16[32,1536]{1,0:T(8,128)(2,1)S(1)}, bf16[32,1536]{1,0:T(8,128)(2,1)S(1)}, u32[]{:S(2)}, u32[]{:S(2)}) collective-permute-start(bf16[32,1536]{1,0:T(8,128)(2,1)S(1)} %slice.33), channel_id=1, source_target_pairs={{0,14},{2,0},{4,2},{6,4},{8,6},{10,8},{12,10},{14,12},{1,15},{3,1}... | collective-permute-start | bytes 294920 | tf_op jit(solution)/shard_map/ppermute | solution.py:349
  104.2 3.3 %collective-permute-start.11 = (bf16[64,1536]{1,0:T(8,128)(2,1)S(1)}, bf16[64,1536]{1,0:T(8,128)(2,1)S(1)}, u32[]{:S(2)}, u32[]{:S(2)}) collective-permute-start(bf16[64,1536]{1,0:T(8,128)(2,1)S(1)} %slice.31), channel_id=1, source_target_pairs={{0,14},{2,0},{4,2},{6,4},{8,6},{10,8},{12,10},{14,12},{1,15},{3,1}... | collective-permute-start | bytes 589832 | tf_op jit(solution)/shard_map/ppermute | solution.py:349
  107.7 3.5 %collective-permute-start.17 = (bf16[16,1536]{1,0:T(8,128)(2,1)S(1)}, bf16[16,1536]{1,0:T(8,128)(2,1)S(1)}, u32[]{:S(2)}, u32[]{:S(2)}) collective-permute-start(bf16[16,1536]{1,0:T(8,128)(2,1)S(1)} %slice.34), channel_id=1, source_target_pairs={{0,14},{2,0},{4,2},{6,4},{8,6},{10,8},{12,10},{14,12},{1,15},{3,1}... | collective-permute-start | bytes 147464 | tf_op jit(solution)/shard_map/ppermute | solution.py:349
  113.0 3.6 %collective-permute-done.19.refs_10_ = bf16[16,1536]{1,0:T(8,128)(2,1)S(1)} collective-permute-done((bf16[16,1536]{1,0:T(8,128)(2,1)S(1)}, bf16[16,1536]{1,0:T(8,128)(2,1)S(1)}, u32[]{:S(2)}, u32[]{:S(2)}) %collective-permute-start.19) | collective-permute-done | bytes 49184 | tf_op jit(solution)/shard_map/ppermute | solution.py:349
  116.6 2.7 project.2
  124.1 7.4 %all-to-all-start.1 = ((bf16[16,384,128]{2,1,0:T(8,128)(2,1)}), bf16[16,384,128]{2,1,0:T(8,128)(2,1)S(1)}, u32[]{:S(2)}, u32[]{:S(2)}) async-start(bf16[16,384,128]{2,1,0:T(8,128)(2,1)} %after.6), calls=%async_computation.1 | async-start | bytes 3145728 | tf_op jit(solution)/shard_map/all_to_all | solution.py:473
  141.4 3.1 %project.3 = (bf16[8,128,128]{2,1,0:T(8,128)(2,1)S(1)}, bf16[8,128,128]{2,1,0:T(8,128)(2,1)S(1)}, bf16[1024,1536]{1,0:T(8,128)(2,1)S(1)}) custom-call(bf16[128,1536]{1,0:T(8,128)(2,1)S(1)} %bitcast.46, bf16[128,1536]{1,0:T(8,128)(2,1)S(1)} %copy-done.11, bf16[128,1536]{1,0:T(8,128)(2,1)} %collective-permute-done.refs_2_, bf16[128,1536]{1,0:T(8,128)(2,1)S(1)} %copy-done.24, ...), custom_call_target="tpu_custom_call" | custom-call | flops 1000 | bytes 1000 | tf_op jit(solution)/shard_map/project/pallas_call | solution.py:75
  147.6 2.6 collective-permute-start.23
  150.2 10.3 %attend.3 = (bf16[8,32,128]{2,1,0:T(8,128)(2,1)}, bf16[8,32,128]{2,1,0:T(8,128)(2,1)S(1)}, bf16[16,384,128]{2,1,0:T(8,128)(2,1)S(1)}) custom-call(s32[6]{0:T(128)S(1)} %pad_add_fusion.1.rows_ref, bf16[16,480,128]{2,1,0:T(8,128)(2,1)S(1)} %all-to-all-done.x_ref, bf16[8,32,128]{2,1,0:T(8,128)(2,1)S(1)} %copy-done.36, bf16[8,32,128]{2,1,0:T(8,128)(2,1)S(1)} %copy-done.38), custom_call_target="tpu_custom_call" | custom-call | tf_op jit(solution)/shard_map/attend/pallas_call | solution.py:320
  162.3 6.7 %collective-permute-done.23.f_ref.refs_2_ = bf16[8,128,128]{2,1,0:T(8,128)(2,1)} collective-permute-done((bf16[8,128,128]{2,1,0:T(8,128)(2,1)S(1)}, bf16[8,128,128]{2,1,0:T(8,128)(2,1)}, u32[]{:S(2)}, u32[]{:S(2)}) %collective-permute-start.23) | collective-permute-done | bytes 262176 | tf_op jit(solution)/shard_map/ppermute | solution.py:386
  170.4 15.6 %all-to-all-start.2 = ((bf16[16,384,128]{2,1,0:T(8,128)(2,1)}), bf16[16,384,128]{2,1,0:T(8,128)(2,1)S(1)}, u32[]{:S(2)}, u32[]{:S(2)}) async-start(bf16[16,384,128]{2,1,0:T(8,128)(2,1)} %after.7), calls=%async_computation.2 | async-start | bytes 3145728 | tf_op jit(solution)/shard_map/all_to_all | solution.py:479
  186.2 34.4 %attend.2 = (bf16[8,128,128]{2,1,0:T(8,128)(2,1)S(1)}, bf16[8,128,128]{2,1,0:T(8,128)(2,1)S(1)}, bf16[16,384,128]{2,1,0:T(8,128)(2,1)S(1)}) custom-call(s32[18]{0:T(128)S(1)} %pad_add_fusion.rows_ref, bf16[16,384,128]{2,1,0:T(8,128)(2,1)S(1)} %all-to-all-done.1.x_ref, bf16[8,128,128]{2,1,0:T(8,128)(2,1)} %collective-permute-done.22.d_ref.refs_1_, ...), custom_call_target="tpu_custom_call" | custom-call | tf_op jit(solution)/shard_map/attend/pallas_call | solution.py:320
  225.9 6.7 %all-to-all-start.3 = ((bf16[16,384,128]{2,1,0:T(8,128)(2,1)}), bf16[16,384,128]{2,1,0:T(8,128)(2,1)S(1)}, u32[]{:S(2)}, u32[]{:S(2)}) async-start(bf16[16,384,128]{2,1,0:T(8,128)(2,1)} %after.8), calls=%async_computation.3 | async-start | bytes 3145728 | tf_op jit(solution)/shard_map/all_to_all | solution.py:485
  241.0 5.3 %collective-permute-done.27.refs_3_ = bf16[8,32,128]{2,1,0:T(8,128)(2,1)S(1)} collective-permute-done((bf16[8,32,128]{2,1,0:T(8,128)(2,1)}, bf16[8,32,128]{2,1,0:T(8,128)(2,1)S(1)}, u32[]{:S(2)}, u32[]{:S(2)}) %collective-permute-start.27) | collective-permute-done | bytes 65568 | tf_op jit(solution)/shard_map/ppermute | solution.py:386
  249.0 3.1 %outer.1 = (f32[128,1536]{1,0:T(8,128)S(1)}, f32[128,1536]{1,0:T(8,128)}) custom-call(bf16[8,128,128]{2,1,0:T(8,128)(2,1)S(1)} %collective-permute-done.24.refs_0_, bf16[8,128,128]{2,1,0:T(8,128)(2,1)} %collective-permute-done.25.refs_1_, bf16[8,32,128]{2,1,0:T(8,128)(2,1)S(1)} %copy-done.40, bf16[8,32,128]{2,1,0:T(8,128)(2,1)S(1)} %collective-permute-done.27.refs_3_, ...), custom_call_target="tpu_custom_call" | custom-call | flops 1000 | bytes 1000 | tf_op jit(solution)/shard_map/outer/pallas_call | solution.py:75
  252.1 2.5 collective-permute-done.28
  261.6 3.0 %collective-permute-done.29 = f32[2,2,8,1536]{3,2,1,0:T(8,128)S(1)} collective-permute-done((f32[2,2,8,1536]{3,2,1,0:T(8,128)S(1)}, f32[2,2,8,1536]{3,2,1,0:T(8,128)S(1)}, u32[]{:S(2)}, u32[]{:S(2)}) %collective-permute-start.29) | collective-permute-done | bytes 196640 | tf_op jit(solution)/shard_map/ppermute | solution.py:349
  264.6 3.1 %collective-permute-done.30 = f32[2,2,8,1536]{3,2,1,0:T(8,128)S(1)} collective-permute-done((f32[2,2,8,1536]{3,2,1,0:T(8,128)S(1)}, f32[2,2,8,1536]{3,2,1,0:T(8,128)S(1)}, u32[]{:S(2)}, u32[]{:S(2)}) %collective-permute-start.30) | collective-permute-done | bytes 196640 | tf_op jit(solution)/shard_map/ppermute | solution.py:349
  270.8 2.9 %collective-permute-start.33 = (f32[8,1536]{1,0:T(8,128)S(1)}, f32[8,1536]{1,0:T(8,128)S(1)}, u32[]{:S(2)}, u32[]{:S(2)}) collective-permute-start(f32[8,1536]{1,0:T(8,128)S(1)} %get-tuple-element.39), channel_id=1, source_target_pairs={{0,16},{1,0},{16,17},{17,1},{128,144},{129,128},{144,145},{145,129... | collective-permute-start | bytes 147464 | tf_op jit(solution)/shard_map/ppermute | solution.py:444
  273.7 2.9 %collective-permute-start.34 = (f32[8,1536]{1,0:T(8,128)S(1)}, f32[8,1536]{1,0:T(8,128)S(1)}, u32[]{:S(2)}, u32[]{:S(2)}) collective-permute-start(f32[8,1536]{1,0:T(8,128)S(1)} %get-tuple-element.41), channel_id=1, source_target_pairs={{0,128},{1,144},{16,129},{17,145},{128,0},{129,16},{144,1},{145,17... | collective-permute-start | bytes 147464 | tf_op jit(solution)/shard_map/ppermute | solution.py:444
  276.6 2.7 collective-permute-done.34
  279.3 2.6 collective-permute-done.35
  (189 shorter events, 76.7 us)
Async XLA Ops:
  8.2 57.6 %all-to-all-start = ((bf16[16,480,128]{2,1,0:T(8,128)(2,1)}), bf16[16,480,128]{2,1,0:T(8,128)(2,1)S(1)}, u32[]{:S(2)}, u32[]{:S(2)}) async-start(bf16[16,480,128]{2,1,0:T(8,128)(2,1)} %copy-done.22), calls=%async_computation | async-start | bytes 3932160 | tf_op jit(solution)/shard_map/all_to_all | solution.py:462
  18.7 8.2 %collective-permute-start.4 = (bf16[8,1536]{1,0:T(8,128)(2,1)S(1)}, bf16[8,1536]{1,0:T(8,128)(2,1)S(1)}, u32[]{:S(2)}, u32[]{:S(2)}) collective-permute-start(bf16[8,1536]{1,0:T(8,128)(2,1)S(1)} %collective-permute-done.3), channel_id=1, source_target_pairs={{0,1},{1,0},{2,3},{3,2},{4,5},{5,4},{6,7},{7,6},{8,9},{9,8},{10,11... | collective-permute-start | bytes 73736 | tf_op jit(solution)/shard_map/ppermute | solution.py:408
  26.9 5.7 %collective-permute-start.5 = (bf16[16,1536]{1,0:T(8,128)(2,1)S(1)}, bf16[16,1536]{1,0:T(8,128)(2,1)S(1)}, u32[]{:S(2)}, u32[]{:S(2)}) collective-permute-start(bf16[16,1536]{1,0:T(8,128)(2,1)S(1)} %pad_maximum_fusion.5), channel_id=1, source_target_pairs={{0,128},{128,0},{1,129},{129,1},{2,130},{130,2},{3,131},{131,3},{4... | collective-permute-start | bytes 147464 | tf_op jit(solution)/shard_map/ppermute | solution.py:408
  29.9 16.9 %collective-permute-start = (bf16[128,1536]{1,0:T(8,128)(2,1)S(1)}, bf16[128,1536]{1,0:T(8,128)(2,1)}, u32[]{:S(2)}, u32[]{:S(2)}) collective-permute-start(bf16[128,1536]{1,0:T(8,128)(2,1)S(1)} %get-tuple-element.18), channel_id=1, source_target_pairs={{0,0},{1,16},{16,1},{17,17},{2,2},{3,18},{18,3},{19,19},{4,4},{5,2... | collective-permute-start | bytes 1179656 | tf_op jit(solution)/shard_map/ppermute | solution.py:344
  32.6 5.6 %collective-permute-start.6 = (bf16[32,1536]{1,0:T(8,128)(2,1)S(1)}, bf16[32,1536]{1,0:T(8,128)(2,1)S(1)}, u32[]{:S(2)}, u32[]{:S(2)}) collective-permute-start(bf16[32,1536]{1,0:T(8,128)(2,1)S(1)} %pad_maximum_fusion.4), channel_id=1, source_target_pairs={{0,32},{32,0},{64,96},{96,64},{1,33},{33,1},{65,97},{97,65},{2,34}... | collective-permute-start | bytes 294920 | tf_op jit(solution)/shard_map/ppermute | solution.py:408
  38.2 8.3 %collective-permute-start.7 = (bf16[64,1536]{1,0:T(8,128)(2,1)S(1)}, bf16[64,1536]{1,0:T(8,128)(2,1)S(1)}, u32[]{:S(2)}, u32[]{:S(2)}) collective-permute-start(bf16[64,1536]{1,0:T(8,128)(2,1)S(1)} %pad_maximum_fusion.3), channel_id=1, source_target_pairs={{0,64},{32,96},{64,0},{96,32},{1,65},{33,97},{65,1},{97,33},{2,66}... | collective-permute-start | bytes 589832 | tf_op jit(solution)/shard_map/ppermute | solution.py:408
  46.7 24.3 %collective-permute-start.8 = (bf16[128,1536]{1,0:T(8,128)(2,1)S(1)}, bf16[128,1536]{1,0:T(8,128)(2,1)S(1)}, u32[]{:S(2)}, u32[]{:S(2)}) collective-permute-start(bf16[128,1536]{1,0:T(8,128)(2,1)S(1)} %bitcast.44), channel_id=1, source_target_pairs={{0,16},{16,0},{1,17},{17,1},{2,18},{18,2},{3,19},{19,3},{4,20},{20... | collective-permute-start | bytes 1179656 | tf_op jit(solution)/shard_map/ppermute | solution.py:349
  46.8 25.0 %collective-permute-start.1 = (bf16[128,1536]{1,0:T(8,128)(2,1)}, bf16[128,1536]{1,0:T(8,128)(2,1)S(1)}, u32[]{:S(2)}, u32[]{:S(2)}) collective-permute-start(bf16[128,1536]{1,0:T(8,128)(2,1)} %collective-permute-done.refs_2_), channel_id=1, source_target_pairs={{0,14},{2,0},{4,2},{6,4},{8,6},{10,8},{12,10},{14,12},{1,15},{3,1}... | collective-permute-start | bytes 1179656 | tf_op jit(solution)/shard_map/ppermute | solution.py:349
  49.5 22.5 %collective-permute-start.12 = (bf16[128,1536]{1,0:T(8,128)(2,1)}, bf16[128,1536]{1,0:T(8,128)(2,1)S(1)}, u32[]{:S(2)}, u32[]{:S(2)}) collective-permute-start(bf16[128,1536]{1,0:T(8,128)(2,1)} %collective-permute-done.refs_2_), channel_id=1, source_target_pairs={{0,2},{2,4},{4,6},{6,8},{8,10},{10,12},{12,14},{14,0},{1,3},{3,5},... | collective-permute-start | bytes 1179656 | tf_op jit(solution)/shard_map/ppermute | solution.py:349
  73.1 13.0 %collective-permute-start.9 = (bf16[160,1536]{1,0:T(8,128)(2,1)S(1)}, bf16[160,1536]{1,0:T(8,128)(2,1)S(1)}, u32[]{:S(2)}, u32[]{:S(2)}) collective-permute-start(bf16[160,1536]{1,0:T(8,128)(2,1)S(1)} %get-tuple-element.46), channel_id=1, source_target_pairs={{0,14},{2,0},{4,2},{6,4},{8,6},{10,8},{12,10},{14,12},{1,15},{3,1}... | collective-permute-start | bytes 1474568 | tf_op jit(solution)/shard_map/ppermute | solution.py:349
  74.6 14.7 %collective-permute-start.13 = (bf16[160,1536]{1,0:T(8,128)(2,1)S(1)}, bf16[160,1536]{1,0:T(8,128)(2,1)S(1)}, u32[]{:S(2)}, u32[]{:S(2)}) collective-permute-start(bf16[160,1536]{1,0:T(8,128)(2,1)S(1)} %get-tuple-element.45), channel_id=1, source_target_pairs={{0,2},{2,4},{4,6},{6,8},{8,10},{10,12},{12,14},{14,0},{1,3},{3,5},... | collective-permute-start | bytes 1474568 | tf_op jit(solution)/shard_map/ppermute | solution.py:349
  86.1 14.3 %collective-permute-start.10 = (bf16[160,1536]{1,0:T(8,128)(2,1)S(1)}, bf16[160,1536]{1,0:T(8,128)(2,1)S(1)}, u32[]{:S(2)}, u32[]{:S(2)}) collective-permute-start(bf16[160,1536]{1,0:T(8,128)(2,1)S(1)} %collective-permute-done.9.refs_3_.refs_4_), channel_id=1, source_target_pairs={{0,14},{2,0},{4,2},{6,4},{8,6},{10,8},{12,10},{14,12},{1,15},{3,1}... | collective-permute-start | bytes 1474568 | tf_op jit(solution)/shard_map/ppermute | solution.py:349
  89.3 14.8 %collective-permute-start.14 = (bf16[160,1536]{1,0:T(8,128)(2,1)S(1)}, bf16[160,1536]{1,0:T(8,128)(2,1)S(1)}, u32[]{:S(2)}, u32[]{:S(2)}) collective-permute-start(bf16[160,1536]{1,0:T(8,128)(2,1)S(1)} %collective-permute-done.13.refs_7_.refs_8_), channel_id=1, source_target_pairs={{0,2},{2,4},{4,6},{6,8},{8,10},{10,12},{12,14},{14,0},{1,3},{3,5},... | collective-permute-start | bytes 1474568 | tf_op jit(solution)/shard_map/ppermute | solution.py:349
  100.3 7.3 %collective-permute-start.16 = (bf16[32,1536]{1,0:T(8,128)(2,1)S(1)}, bf16[32,1536]{1,0:T(8,128)(2,1)S(1)}, u32[]{:S(2)}, u32[]{:S(2)}) collective-permute-start(bf16[32,1536]{1,0:T(8,128)(2,1)S(1)} %slice.33), channel_id=1, source_target_pairs={{0,14},{2,0},{4,2},{6,4},{8,6},{10,8},{12,10},{14,12},{1,15},{3,1}... | collective-permute-start | bytes 294920 | tf_op jit(solution)/shard_map/ppermute | solution.py:349
  104.1 7.1 %collective-permute-start.18 = (bf16[32,1536]{1,0:T(8,128)(2,1)S(1)}, bf16[32,1536]{1,0:T(8,128)(2,1)S(1)}, u32[]{:S(2)}, u32[]{:S(2)}) collective-permute-start(bf16[32,1536]{1,0:T(8,128)(2,1)S(1)} %slice.35), channel_id=1, source_target_pairs={{0,2},{2,4},{4,6},{6,8},{8,10},{10,12},{12,14},{14,0},{1,3},{3,5},... | collective-permute-start | bytes 294920 | tf_op jit(solution)/shard_map/ppermute | solution.py:349
  104.2 18.4 %collective-permute-start.11 = (bf16[64,1536]{1,0:T(8,128)(2,1)S(1)}, bf16[64,1536]{1,0:T(8,128)(2,1)S(1)}, u32[]{:S(2)}, u32[]{:S(2)}) collective-permute-start(bf16[64,1536]{1,0:T(8,128)(2,1)S(1)} %slice.31), channel_id=1, source_target_pairs={{0,14},{2,0},{4,2},{6,4},{8,6},{10,8},{12,10},{14,12},{1,15},{3,1}... | collective-permute-start | bytes 589832 | tf_op jit(solution)/shard_map/ppermute | solution.py:349
  107.6 15.1 %collective-permute-start.15 = (bf16[64,1536]{1,0:T(8,128)(2,1)S(1)}, bf16[64,1536]{1,0:T(8,128)(2,1)S(1)}, u32[]{:S(2)}, u32[]{:S(2)}) collective-permute-start(bf16[64,1536]{1,0:T(8,128)(2,1)S(1)} %slice.32), channel_id=1, source_target_pairs={{0,2},{2,4},{4,6},{6,8},{8,10},{10,12},{12,14},{14,0},{1,3},{3,5},... | collective-permute-start | bytes 589832 | tf_op jit(solution)/shard_map/ppermute | solution.py:349
  111.2 5.4 %collective-permute-start.19 = (bf16[16,1536]{1,0:T(8,128)(2,1)S(1)}, bf16[16,1536]{1,0:T(8,128)(2,1)S(1)}, u32[]{:S(2)}, u32[]{:S(2)}) collective-permute-start(bf16[16,1536]{1,0:T(8,128)(2,1)S(1)} %slice.36), channel_id=1, source_target_pairs={{0,2},{2,4},{4,6},{6,8},{8,10},{10,12},{12,14},{14,0},{1,3},{3,5},... | collective-permute-start | bytes 147464 | tf_op jit(solution)/shard_map/ppermute | solution.py:349
  124.1 46.3 %all-to-all-start.1 = ((bf16[16,384,128]{2,1,0:T(8,128)(2,1)}), bf16[16,384,128]{2,1,0:T(8,128)(2,1)S(1)}, u32[]{:S(2)}, u32[]{:S(2)}) async-start(bf16[16,384,128]{2,1,0:T(8,128)(2,1)} %after.6), calls=%async_computation.1 | async-start | bytes 3145728 | tf_op jit(solution)/shard_map/all_to_all | solution.py:473
  146.2 16.1 %collective-permute-start.22 = (bf16[8,128,128]{2,1,0:T(8,128)(2,1)S(1)}, bf16[8,128,128]{2,1,0:T(8,128)(2,1)}, u32[]{:S(2)}, u32[]{:S(2)}) collective-permute-start(bf16[8,128,128]{2,1,0:T(8,128)(2,1)S(1)} %get-tuple-element.22), channel_id=1, source_target_pairs={{0,0},{1,16},{16,1},{17,17},{2,2},{3,18},{18,3},{19,19},{4,4},{5,2... | collective-permute-start | bytes 786440 | tf_op jit(solution)/shard_map/ppermute | solution.py:386
  147.6 21.4 %collective-permute-start.23 = (bf16[8,128,128]{2,1,0:T(8,128)(2,1)S(1)}, bf16[8,128,128]{2,1,0:T(8,128)(2,1)}, u32[]{:S(2)}, u32[]{:S(2)}) collective-permute-start(bf16[8,128,128]{2,1,0:T(8,128)(2,1)S(1)} %get-tuple-element.23), channel_id=1, source_target_pairs={{0,1},{1,17},{16,0},{17,16},{2,3},{3,19},{18,2},{19,18},{4,5},{5,2... | collective-permute-start | bytes 786440 | tf_op jit(solution)/shard_map/ppermute | solution.py:386
  170.4 54.4 %all-to-all-start.2 = ((bf16[16,384,128]{2,1,0:T(8,128)(2,1)}), bf16[16,384,128]{2,1,0:T(8,128)(2,1)S(1)}, u32[]{:S(2)}, u32[]{:S(2)}) async-start(bf16[16,384,128]{2,1,0:T(8,128)(2,1)} %after.7), calls=%async_computation.2 | async-start | bytes 3145728 | tf_op jit(solution)/shard_map/all_to_all | solution.py:479
  225.9 56.6 %all-to-all-start.3 = ((bf16[16,384,128]{2,1,0:T(8,128)(2,1)}), bf16[16,384,128]{2,1,0:T(8,128)(2,1)S(1)}, u32[]{:S(2)}, u32[]{:S(2)}) async-start(bf16[16,384,128]{2,1,0:T(8,128)(2,1)} %after.8), calls=%async_computation.3 | async-start | bytes 3145728 | tf_op jit(solution)/shard_map/all_to_all | solution.py:485
  232.7 13.6 %collective-permute-start.24 = (bf16[8,128,128]{2,1,0:T(8,128)(2,1)}, bf16[8,128,128]{2,1,0:T(8,128)(2,1)S(1)}, u32[]{:S(2)}, u32[]{:S(2)}) collective-permute-start(bf16[8,128,128]{2,1,0:T(8,128)(2,1)} %copy-done.44), channel_id=1, source_target_pairs={{0,0},{16,1},{1,16},{17,17},{2,2},{18,3},{3,18},{19,19},{4,4},{20,... | collective-permute-start | bytes 786440 | tf_op jit(solution)/shard_map/ppermute | solution.py:386
  234.3 12.0 %collective-permute-start.25 = (bf16[8,128,128]{2,1,0:T(8,128)(2,1)}, bf16[8,128,128]{2,1,0:T(8,128)(2,1)}, u32[]{:S(2)}, u32[]{:S(2)}) collective-permute-start(bf16[8,128,128]{2,1,0:T(8,128)(2,1)} %copy-done.43), channel_id=1, source_target_pairs={{1,0},{17,1},{0,16},{16,17},{3,2},{19,3},{2,18},{18,19},{5,4},{21,... | collective-permute-start | bytes 786440 | tf_op jit(solution)/shard_map/ppermute | solution.py:386
  238.2 8.1 %collective-permute-start.27 = (bf16[8,32,128]{2,1,0:T(8,128)(2,1)}, bf16[8,32,128]{2,1,0:T(8,128)(2,1)S(1)}, u32[]{:S(2)}, u32[]{:S(2)}) collective-permute-start(bf16[8,32,128]{2,1,0:T(8,128)(2,1)} %copy-done.45), channel_id=1, source_target_pairs={{1,0},{17,1},{0,16},{16,17},{3,2},{19,3},{2,18},{18,19},{5,4},{21,... | collective-permute-start | bytes 196616 | tf_op jit(solution)/shard_map/ppermute | solution.py:386
  256.8 7.8 %collective-permute-start.29 = (f32[2,2,8,1536]{3,2,1,0:T(8,128)S(1)}, f32[2,2,8,1536]{3,2,1,0:T(8,128)S(1)}, u32[]{:S(2)}, u32[]{:S(2)}) collective-permute-start(f32[2,2,8,1536]{3,2,1,0:T(8,128)S(1)} %get-tuple-element.34), channel_id=1, source_target_pairs={{0,32},{32,64},{64,96},{96,0},{1,33},{33,65},{65,97},{97,1},{2,34}... | collective-permute-start | bytes 589832 | tf_op jit(solution)/shard_map/ppermute | solution.py:349
  258.4 9.3 %collective-permute-start.30 = (f32[2,2,8,1536]{3,2,1,0:T(8,128)S(1)}, f32[2,2,8,1536]{3,2,1,0:T(8,128)S(1)}, u32[]{:S(2)}, u32[]{:S(2)}) collective-permute-start(f32[2,2,8,1536]{3,2,1,0:T(8,128)S(1)} %get-tuple-element.36), channel_id=1, source_target_pairs={{0,64},{32,96},{64,0},{96,32},{1,65},{33,97},{65,1},{97,33},{2,66}... | collective-permute-start | bytes 589832 | tf_op jit(solution)/shard_map/ppermute | solution.py:349
  259.4 10.6 %collective-permute-start.31 = (f32[2,2,8,1536]{3,2,1,0:T(8,128)S(1)}, f32[2,2,8,1536]{3,2,1,0:T(8,128)S(1)}, u32[]{:S(2)}, u32[]{:S(2)}) collective-permute-start(f32[2,2,8,1536]{3,2,1,0:T(8,128)S(1)} %get-tuple-element.35), channel_id=1, source_target_pairs={{0,96},{32,0},{64,32},{96,64},{1,97},{33,1},{65,33},{97,65},{2,98}... | collective-permute-start | bytes 589832 | tf_op jit(solution)/shard_map/ppermute | solution.py:349
  270.1 6.5 %collective-permute-start.32 = (f32[8,1536]{1,0:T(8,128)S(1)}, f32[8,1536]{1,0:T(8,128)S(1)}, u32[]{:S(2)}, u32[]{:S(2)}) collective-permute-start(f32[8,1536]{1,0:T(8,128)S(1)} %get-tuple-element.42), channel_id=1, source_target_pairs={{0,0},{1,16},{16,1},{17,17},{128,128},{129,144},{144,129},{145,145... | collective-permute-start | bytes 147464 | tf_op jit(solution)/shard_map/ppermute | solution.py:444
  270.8 5.8 %collective-permute-start.33 = (f32[8,1536]{1,0:T(8,128)S(1)}, f32[8,1536]{1,0:T(8,128)S(1)}, u32[]{:S(2)}, u32[]{:S(2)}) collective-permute-start(f32[8,1536]{1,0:T(8,128)S(1)} %get-tuple-element.39), channel_id=1, source_target_pairs={{0,16},{1,0},{16,17},{17,1},{128,144},{129,128},{144,145},{145,129... | collective-permute-start | bytes 147464 | tf_op jit(solution)/shard_map/ppermute | solution.py:444
  273.7 5.6 %collective-permute-start.34 = (f32[8,1536]{1,0:T(8,128)S(1)}, f32[8,1536]{1,0:T(8,128)S(1)}, u32[]{:S(2)}, u32[]{:S(2)}) collective-permute-start(f32[8,1536]{1,0:T(8,128)S(1)} %get-tuple-element.41), channel_id=1, source_target_pairs={{0,128},{1,144},{16,129},{17,145},{128,0},{129,16},{144,1},{145,17... | collective-permute-start | bytes 147464 | tf_op jit(solution)/shard_map/ppermute | solution.py:444
  (56 other events, 425.3 us)

commit v4 on v3

--- a/solution.py
+++ b/solution.py
@@ -471,12 +471,12 @@
     grads_low = [cross(grads_low[k], k) for k in range(2)]
     sent_one = after(split_heads(qkv, 0, frames), ring_one[4], ring_one[8], *grads_low)
     heads_one = lax.all_to_all(sent_one, seq, 0, 0, tiled=True)
-    *grads, rows_high = project(weight, other, ring_one, first_pieces)
-    grads = [cross(grads[k], k) for k in range(2)]
+    *high_here, rows_high = project(weight, other, ring_one, first_pieces)
+    grads = [cross(high_here[k], k) for k in range(2)]
 
     rows_two = jnp.concatenate([live, place[None], low[None]])
     *out_two, back_two = attend(rows_two, heads_two, grads_low, live_count)
-    grads_two = lax.all_to_all(after(back_two, *grads), seq, 0, 0, tiled=True)
+    grads_two = lax.all_to_all(after(back_two, *high_here), seq, 0, 0, tiled=True)
     out_two = [cross(out_two[k], k, True) for k in range(2)]
 
     every = jnp.arange(frames, dtype=jnp.int32)

time: 290 us -> 299 us (1.031); the launches traced: 284 us -> 296 us
  starting transfers between devices: 97.6 us -> 105 us
  waiting for transfers between devices: 89.7 us -> 95.6 us
    all_to_all x1, starting transfers between devices: 15.6 us -> 3.71 us  [per_device(): lax.all_to_all(after(back_two, *high_here), seq, 0, 0, tiled=True)]
    all_to_all x1, waiting for transfers between devices: 1.44 us -> 12 us  [per_device(): heads_one = lax.all_to_all(sent_one, seq, 0, 0, tiled=True)]
    all_to_all x1, starting transfers between devices: 6.72 us -> 16.3 us  [per_device(): lax.all_to_all(after(back_one, grads_two), seq, 0, 0, tiled=True)]
    ppermute x8, starting transfers between devices: 11.8 us -> 21.3 us  [cross(): lax.ppermute(value, ('co', 'yl'), [p[::-1] for p in pairs] if back else p...]
    ppermute x8, waiting for transfers between devices: 12.4 us -> 9.31 us  [cross(): lax.ppermute(value, ('co', 'yl'), [p[::-1] for p in pairs] if back else p...]
    unnamed x96 -> x102, local copies, waits for them, and re-layouts: 30.1 us -> 30.2 us
  transfers between devices with their start and end apart: 40 -> 40, of which waited for: 22 -> 21; matrix products, arithmetic and copies ran while one was open for 2% -> 2% of each run, Pallas kernels for 20% -> 18%
where the time goes in v4:
time: 299 us; the launch traced here: 296 us
  starting transfers between devices  105 us (35%)
  waiting for transfers between devices  95.6 us (32%)
  Pallas kernels  57.2 us (19%)
  local copies, waits for them, and re-layouts  33.3 us (11%)
  other arithmetic  3.61 us (1%)
    pallas_call x2, Pallas kernels, attend(): pl.pallas_call(functools.partial(attend_kernel, scale=HEAD_DIM ** (-0.5),...  43.8 us
    ppermute x17, waiting for transfers between devices, turn(): lax.ppermute(value, axis, [(i, (i + by) % size) for i in range(size)])  38.7 us
    unnamed x102, local copies, waits for them, and re-layouts  30.2 us
    ppermute x17, starting transfers between devices, turn(): lax.ppermute(value, axis, [(i, (i + by) % size) for i in range(size)])  23.5 us
    ppermute x8, starting transfers between devices, cross(): lax.ppermute(value, ('co', 'yl'), [p[::-1] for p in pairs] if back else p...  21.3 us
    all_to_all x1, waiting for transfers between devices, per_device(): heads_two = lax.all_to_all(sent_two, seq, 0, 0, tiled=True)  16.3 us
    all_to_all x1, starting transfers between devices, per_device(): lax.all_to_all(after(back_one, grads_two), seq, 0, 0, tiled=True)  16.3 us
    ppermute x4, waiting for transfers between devices, gather_pair(): other = lax.ppermute(value, axis, [(i, i ^ bit) for i in range(size)])  13.9 us
  transfers between devices with their start and end apart: 40, of which 21 were waited for; matrix products, arithmetic and copies ran while one was open for 2% of the time, Pallas kernels for 18%

profile of v4, /device:TPU:2, one launch (start us, length us, event | category | flops | bytes accessed | tf_op | source)
XLA Modules:
  0.0 296.5 jit_solution(12370891477700911107)
XLA Ops:
  8.2 9.7 %all-to-all-start = ((bf16[16,480,128]{2,1,0:T(8,128)(2,1)}), bf16[16,480,128]{2,1,0:T(8,128)(2,1)S(1)}, u32[]{:S(2)}, u32[]{:S(2)}) async-start(bf16[16,480,128]{2,1,0:T(8,128)(2,1)} %copy-done.22), calls=%async_computation | async-start | bytes 3932160 | tf_op jit(solution)/shard_map/all_to_all | solution.py:462
  18.7 6.4 %collective-permute-start.4 = (bf16[8,1536]{1,0:T(8,128)(2,1)S(1)}, bf16[8,1536]{1,0:T(8,128)(2,1)S(1)}, u32[]{:S(2)}, u32[]{:S(2)}) collective-permute-start(bf16[8,1536]{1,0:T(8,128)(2,1)S(1)} %collective-permute-done.3), channel_id=1, source_target_pairs={{0,1},{1,0},{2,3},{3,2},{4,5},{5,4},{6,7},{7,6},{8,9},{9,8},{10,11... | collective-permute-start | bytes 73736 | tf_op jit(solution)/shard_map/ppermute | solution.py:408
  26.9 3.0 %collective-permute-start.5 = (bf16[16,1536]{1,0:T(8,128)(2,1)S(1)}, bf16[16,1536]{1,0:T(8,128)(2,1)S(1)}, u32[]{:S(2)}, u32[]{:S(2)}) collective-permute-start(bf16[16,1536]{1,0:T(8,128)(2,1)S(1)} %pad_maximum_fusion.5), channel_id=1, source_target_pairs={{0,128},{128,0},{1,129},{129,1},{2,130},{130,2},{3,131},{131,3},{4... | collective-permute-start | bytes 147464 | tf_op jit(solution)/shard_map/ppermute | solution.py:408
  33.2 4.9 %collective-permute-done.6 = bf16[32,1536]{1,0:T(8,128)(2,1)S(1)} collective-permute-done((bf16[32,1536]{1,0:T(8,128)(2,1)S(1)}, bf16[32,1536]{1,0:T(8,128)(2,1)S(1)}, u32[]{:S(2)}, u32[]{:S(2)}) %collective-permute-start.6) | collective-permute-done | bytes 98336 | tf_op jit(solution)/shard_map/ppermute | solution.py:408
  40.7 5.9 %collective-permute-done.7 = bf16[64,1536]{1,0:T(8,128)(2,1)S(1)} collective-permute-done((bf16[64,1536]{1,0:T(8,128)(2,1)S(1)}, bf16[64,1536]{1,0:T(8,128)(2,1)S(1)}, u32[]{:S(2)}, u32[]{:S(2)}) %collective-permute-start.7) | collective-permute-done | bytes 196640 | tf_op jit(solution)/shard_map/ppermute | solution.py:408
  46.8 2.8 collective-permute-start.1
  49.5 16.3 %all-to-all-done.x_ref = bf16[16,480,128]{2,1,0:T(8,128)(2,1)S(1)} async-done(((bf16[16,480,128]{2,1,0:T(8,128)(2,1)}), bf16[16,480,128]{2,1,0:T(8,128)(2,1)S(1)}, u32[]{:S(2)}, u32[]{:S(2)}) %all-to-all-start) | async-done | bytes 1966112 | tf_op jit(solution)/shard_map/all_to_all | solution.py:462
  75.2 10.9 %collective-permute-done.9.refs_3_.refs_4_ = bf16[160,1536]{1,0:T(8,128)(2,1)S(1)} collective-permute-done((bf16[160,1536]{1,0:T(8,128)(2,1)S(1)}, bf16[160,1536]{1,0:T(8,128)(2,1)S(1)}, u32[]{:S(2)}, u32[]{:S(2)}) %collective-permute-start.9) | collective-permute-done | bytes 491552 | tf_op jit(solution)/shard_map/ppermute | solution.py:349
  86.1 2.8 collective-permute-start.10
  89.3 11.0 %collective-permute-done.10.refs_4_.refs_5_ = bf16[160,1536]{1,0:T(8,128)(2,1)S(1)} collective-permute-done((bf16[160,1536]{1,0:T(8,128)(2,1)S(1)}, bf16[160,1536]{1,0:T(8,128)(2,1)S(1)}, u32[]{:S(2)}, u32[]{:S(2)}) %collective-permute-start.10) | collective-permute-done | bytes 491552 | tf_op jit(solution)/shard_map/ppermute | solution.py:349
  100.3 3.8 %collective-permute-start.16 = (bf16[32,1536]{1,0:T(8,128)(2,1)S(1)}, bf16[32,1536]{1,0:T(8,128)(2,1)S(1)}, u32[]{:S(2)}, u32[]{:S(2)}) collective-permute-start(bf16[32,1536]{1,0:T(8,128)(2,1)S(1)} %slice.33), channel_id=1, source_target_pairs={{0,14},{2,0},{4,2},{6,4},{8,6},{10,8},{12,10},{14,12},{1,15},{3,1}... | collective-permute-start | bytes 294920 | tf_op jit(solution)/shard_map/ppermute | solution.py:349
  104.2 3.3 %collective-permute-start.11 = (bf16[64,1536]{1,0:T(8,128)(2,1)S(1)}, bf16[64,1536]{1,0:T(8,128)(2,1)S(1)}, u32[]{:S(2)}, u32[]{:S(2)}) collective-permute-start(bf16[64,1536]{1,0:T(8,128)(2,1)S(1)} %slice.31), channel_id=1, source_target_pairs={{0,14},{2,0},{4,2},{6,4},{8,6},{10,8},{12,10},{14,12},{1,15},{3,1}... | collective-permute-start | bytes 589832 | tf_op jit(solution)/shard_map/ppermute | solution.py:349
  107.7 3.5 %collective-permute-start.17 = (bf16[16,1536]{1,0:T(8,128)(2,1)S(1)}, bf16[16,1536]{1,0:T(8,128)(2,1)S(1)}, u32[]{:S(2)}, u32[]{:S(2)}) collective-permute-start(bf16[16,1536]{1,0:T(8,128)(2,1)S(1)} %slice.34), channel_id=1, source_target_pairs={{0,14},{2,0},{4,2},{6,4},{8,6},{10,8},{12,10},{14,12},{1,15},{3,1}... | collective-permute-start | bytes 147464 | tf_op jit(solution)/shard_map/ppermute | solution.py:349
  113.0 3.6 %collective-permute-done.19.refs_10_ = bf16[16,1536]{1,0:T(8,128)(2,1)S(1)} collective-permute-done((bf16[16,1536]{1,0:T(8,128)(2,1)S(1)}, bf16[16,1536]{1,0:T(8,128)(2,1)S(1)}, u32[]{:S(2)}, u32[]{:S(2)}) %collective-permute-start.19) | collective-permute-done | bytes 49184 | tf_op jit(solution)/shard_map/ppermute | solution.py:349
  116.6 2.7 project.2
  124.1 7.4 %all-to-all-start.1 = ((bf16[16,384,128]{2,1,0:T(8,128)(2,1)}), bf16[16,384,128]{2,1,0:T(8,128)(2,1)S(1)}, u32[]{:S(2)}, u32[]{:S(2)}) async-start(bf16[16,384,128]{2,1,0:T(8,128)(2,1)} %after.6), calls=%async_computation.1 | async-start | bytes 3145728 | tf_op jit(solution)/shard_map/all_to_all | solution.py:473
  141.5 3.1 %project.3 = (bf16[8,128,128]{2,1,0:T(8,128)(2,1)S(1)}, bf16[8,128,128]{2,1,0:T(8,128)(2,1)S(1)}, bf16[1024,1536]{1,0:T(8,128)(2,1)S(1)}) custom-call(bf16[128,1536]{1,0:T(8,128)(2,1)S(1)} %bitcast.46, bf16[128,1536]{1,0:T(8,128)(2,1)S(1)} %copy-done.11, bf16[128,1536]{1,0:T(8,128)(2,1)} %collective-permute-done.refs_2_, bf16[128,1536]{1,0:T(8,128)(2,1)S(1)} %copy-done.24, ...), custom_call_target="tpu_custom_call" | custom-call | flops 1000 | bytes 1000 | tf_op jit(solution)/shard_map/project/pallas_call | solution.py:75
  146.3 10.3 %attend.3 = (bf16[8,32,128]{2,1,0:T(8,128)(2,1)}, bf16[8,32,128]{2,1,0:T(8,128)(2,1)S(1)}, bf16[16,384,128]{2,1,0:T(8,128)(2,1)S(1)}) custom-call(s32[6]{0:T(128)S(1)} %pad_add_fusion.1.rows_ref, bf16[16,480,128]{2,1,0:T(8,128)(2,1)S(1)} %all-to-all-done.x_ref, bf16[8,32,128]{2,1,0:T(8,128)(2,1)S(1)} %copy-done.36, bf16[8,32,128]{2,1,0:T(8,128)(2,1)S(1)} %copy-done.38), custom_call_target="tpu_custom_call" | custom-call | tf_op jit(solution)/shard_map/attend/pallas_call | solution.py:320
  158.5 12.0 %all-to-all-done.1.x_ref = bf16[16,384,128]{2,1,0:T(8,128)(2,1)S(1)} async-done(((bf16[16,384,128]{2,1,0:T(8,128)(2,1)}), bf16[16,384,128]{2,1,0:T(8,128)(2,1)S(1)}, u32[]{:S(2)}, u32[]{:S(2)}) %all-to-all-start.1) | async-done | bytes 1572896 | tf_op jit(solution)/shard_map/all_to_all | solution.py:473
  170.5 3.7 %all-to-all-start.2 = ((bf16[16,384,128]{2,1,0:T(8,128)(2,1)}), bf16[16,384,128]{2,1,0:T(8,128)(2,1)S(1)}, u32[]{:S(2)}, u32[]{:S(2)}) async-start(bf16[16,384,128]{2,1,0:T(8,128)(2,1)} %after.7), calls=%async_computation.2 | async-start | bytes 3145728 | tf_op jit(solution)/shard_map/all_to_all | solution.py:479
  175.8 11.9 %collective-permute-start.23 = (bf16[8,128,128]{2,1,0:T(8,128)(2,1)S(1)}, bf16[8,128,128]{2,1,0:T(8,128)(2,1)S(1)}, u32[]{:S(2)}, u32[]{:S(2)}) collective-permute-start(bf16[8,128,128]{2,1,0:T(8,128)(2,1)S(1)} %copy-done.42), channel_id=1, source_target_pairs={{0,1},{1,17},{16,0},{17,16},{2,3},{3,19},{18,2},{19,18},{4,5},{5,2... | collective-permute-start | bytes 786440 | tf_op jit(solution)/shard_map/ppermute | solution.py:386
  187.8 4.3 %collective-permute-done.23.f_ref = bf16[8,128,128]{2,1,0:T(8,128)(2,1)S(1)} collective-permute-done((bf16[8,128,128]{2,1,0:T(8,128)(2,1)S(1)}, bf16[8,128,128]{2,1,0:T(8,128)(2,1)S(1)}, u32[]{:S(2)}, u32[]{:S(2)}) %collective-permute-start.23) | collective-permute-done | bytes 262176 | tf_op jit(solution)/shard_map/ppermute | solution.py:386
  192.0 33.5 %attend.2 = (bf16[8,128,128]{2,1,0:T(8,128)(2,1)S(1)}, bf16[8,128,128]{2,1,0:T(8,128)(2,1)S(1)}, bf16[16,384,128]{2,1,0:T(8,128)(2,1)S(1)}) custom-call(s32[18]{0:T(128)S(1)} %pad_add_fusion.rows_ref, bf16[16,384,128]{2,1,0:T(8,128)(2,1)S(1)} %all-to-all-done.1.x_ref, bf16[8,128,128]{2,1,0:T(8,128)(2,1)S(1)} %collective-permute-done.22.d_ref, ...), custom_call_target="tpu_custom_call" | custom-call | tf_op jit(solution)/shard_map/attend/pallas_call | solution.py:320
  229.3 16.3 %all-to-all-start.3 = ((bf16[16,384,128]{2,1,0:T(8,128)(2,1)}), bf16[16,384,128]{2,1,0:T(8,128)(2,1)S(1)}, u32[]{:S(2)}, u32[]{:S(2)}) async-start(bf16[16,384,128]{2,1,0:T(8,128)(2,1)} %after.8), calls=%async_computation.3 | async-start | bytes 3145728 | tf_op jit(solution)/shard_map/all_to_all | solution.py:485
  253.8 4.6 %collective-permute-done.27.refs_3_ = bf16[8,32,128]{2,1,0:T(8,128)(2,1)S(1)} collective-permute-done((bf16[8,32,128]{2,1,0:T(8,128)(2,1)}, bf16[8,32,128]{2,1,0:T(8,128)(2,1)S(1)}, u32[]{:S(2)}, u32[]{:S(2)}) %collective-permute-start.27) | collective-permute-done | bytes 65568 | tf_op jit(solution)/shard_map/ppermute | solution.py:386
  261.2 3.1 %outer.1 = (f32[128,1536]{1,0:T(8,128)S(1)}, f32[128,1536]{1,0:T(8,128)}) custom-call(bf16[8,128,128]{2,1,0:T(8,128)(2,1)S(1)} %collective-permute-done.24.refs_0_, bf16[8,128,128]{2,1,0:T(8,128)(2,1)} %collective-permute-done.25.refs_1_, bf16[8,32,128]{2,1,0:T(8,128)(2,1)S(1)} %copy-done.40, bf16[8,32,128]{2,1,0:T(8,128)(2,1)S(1)} %collective-permute-done.27.refs_3_, ...), custom_call_target="tpu_custom_call" | custom-call | flops 1000 | bytes 1000 | tf_op jit(solution)/shard_map/outer/pallas_call | solution.py:75
  273.7 3.0 %collective-permute-done.29 = f32[2,2,8,1536]{3,2,1,0:T(8,128)S(1)} collective-permute-done((f32[2,2,8,1536]{3,2,1,0:T(8,128)S(1)}, f32[2,2,8,1536]{3,2,1,0:T(8,128)S(1)}, u32[]{:S(2)}, u32[]{:S(2)}) %collective-permute-start.29) | collective-permute-done | bytes 196640 | tf_op jit(solution)/shard_map/ppermute | solution.py:349
  276.7 3.0 %collective-permute-done.30 = f32[2,2,8,1536]{3,2,1,0:T(8,128)S(1)} collective-permute-done((f32[2,2,8,1536]{3,2,1,0:T(8,128)S(1)}, f32[2,2,8,1536]{3,2,1,0:T(8,128)S(1)}, u32[]{:S(2)}, u32[]{:S(2)}) %collective-permute-start.30) | collective-permute-done | bytes 196640 | tf_op jit(solution)/shard_map/ppermute | solution.py:349
  282.9 3.0 %collective-permute-start.33 = (f32[8,1536]{1,0:T(8,128)S(1)}, f32[8,1536]{1,0:T(8,128)S(1)}, u32[]{:S(2)}, u32[]{:S(2)}) collective-permute-start(f32[8,1536]{1,0:T(8,128)S(1)} %get-tuple-element.39), channel_id=1, source_target_pairs={{0,16},{1,0},{16,17},{17,1},{128,144},{129,128},{144,145},{145,129... | collective-permute-start | bytes 147464 | tf_op jit(solution)/shard_map/ppermute | solution.py:444
  285.9 2.9 collective-permute-start.34
  288.8 2.7 collective-permute-done.34
  291.5 2.6 collective-permute-done.35
  (195 shorter events, 76.5 us)
Async XLA Ops:
  8.2 57.6 %all-to-all-start = ((bf16[16,480,128]{2,1,0:T(8,128)(2,1)}), bf16[16,480,128]{2,1,0:T(8,128)(2,1)S(1)}, u32[]{:S(2)}, u32[]{:S(2)}) async-start(bf16[16,480,128]{2,1,0:T(8,128)(2,1)} %copy-done.22), calls=%async_computation | async-start | bytes 3932160 | tf_op jit(solution)/shard_map/all_to_all | solution.py:462
  18.7 8.2 %collective-permute-start.4 = (bf16[8,1536]{1,0:T(8,128)(2,1)S(1)}, bf16[8,1536]{1,0:T(8,128)(2,1)S(1)}, u32[]{:S(2)}, u32[]{:S(2)}) collective-permute-start(bf16[8,1536]{1,0:T(8,128)(2,1)S(1)} %collective-permute-done.3), channel_id=1, source_target_pairs={{0,1},{1,0},{2,3},{3,2},{4,5},{5,4},{6,7},{7,6},{8,9},{9,8},{10,11... | collective-permute-start | bytes 73736 | tf_op jit(solution)/shard_map/ppermute | solution.py:408
  26.9 5.7 %collective-permute-start.5 = (bf16[16,1536]{1,0:T(8,128)(2,1)S(1)}, bf16[16,1536]{1,0:T(8,128)(2,1)S(1)}, u32[]{:S(2)}, u32[]{:S(2)}) collective-permute-start(bf16[16,1536]{1,0:T(8,128)(2,1)S(1)} %pad_maximum_fusion.5), channel_id=1, source_target_pairs={{0,128},{128,0},{1,129},{129,1},{2,130},{130,2},{3,131},{131,3},{4... | collective-permute-start | bytes 147464 | tf_op jit(solution)/shard_map/ppermute | solution.py:408
  29.9 16.9 %collective-permute-start = (bf16[128,1536]{1,0:T(8,128)(2,1)S(1)}, bf16[128,1536]{1,0:T(8,128)(2,1)}, u32[]{:S(2)}, u32[]{:S(2)}) collective-permute-start(bf16[128,1536]{1,0:T(8,128)(2,1)S(1)} %get-tuple-element.18), channel_id=1, source_target_pairs={{0,0},{1,16},{16,1},{17,17},{2,2},{3,18},{18,3},{19,19},{4,4},{5,2... | collective-permute-start | bytes 1179656 | tf_op jit(solution)/shard_map/ppermute | solution.py:344
  32.6 5.6 %collective-permute-start.6 = (bf16[32,1536]{1,0:T(8,128)(2,1)S(1)}, bf16[32,1536]{1,0:T(8,128)(2,1)S(1)}, u32[]{:S(2)}, u32[]{:S(2)}) collective-permute-start(bf16[32,1536]{1,0:T(8,128)(2,1)S(1)} %pad_maximum_fusion.4), channel_id=1, source_target_pairs={{0,32},{32,0},{64,96},{96,64},{1,33},{33,1},{65,97},{97,65},{2,34}... | collective-permute-start | bytes 294920 | tf_op jit(solution)/shard_map/ppermute | solution.py:408
  38.2 8.3 %collective-permute-start.7 = (bf16[64,1536]{1,0:T(8,128)(2,1)S(1)}, bf16[64,1536]{1,0:T(8,128)(2,1)S(1)}, u32[]{:S(2)}, u32[]{:S(2)}) collective-permute-start(bf16[64,1536]{1,0:T(8,128)(2,1)S(1)} %pad_maximum_fusion.3), channel_id=1, source_target_pairs={{0,64},{32,96},{64,0},{96,32},{1,65},{33,97},{65,1},{97,33},{2,66}... | collective-permute-start | bytes 589832 | tf_op jit(solution)/shard_map/ppermute | solution.py:408
  46.7 24.3 %collective-permute-start.8 = (bf16[128,1536]{1,0:T(8,128)(2,1)S(1)}, bf16[128,1536]{1,0:T(8,128)(2,1)S(1)}, u32[]{:S(2)}, u32[]{:S(2)}) collective-permute-start(bf16[128,1536]{1,0:T(8,128)(2,1)S(1)} %bitcast.44), channel_id=1, source_target_pairs={{0,16},{16,0},{1,17},{17,1},{2,18},{18,2},{3,19},{19,3},{4,20},{20... | collective-permute-start | bytes 1179656 | tf_op jit(solution)/shard_map/ppermute | solution.py:349
  46.8 25.0 %collective-permute-start.1 = (bf16[128,1536]{1,0:T(8,128)(2,1)}, bf16[128,1536]{1,0:T(8,128)(2,1)S(1)}, u32[]{:S(2)}, u32[]{:S(2)}) collective-permute-start(bf16[128,1536]{1,0:T(8,128)(2,1)} %collective-permute-done.refs_2_), channel_id=1, source_target_pairs={{0,14},{2,0},{4,2},{6,4},{8,6},{10,8},{12,10},{14,12},{1,15},{3,1}... | collective-permute-start | bytes 1179656 | tf_op jit(solution)/shard_map/ppermute | solution.py:349
  49.5 22.5 %collective-permute-start.12 = (bf16[128,1536]{1,0:T(8,128)(2,1)}, bf16[128,1536]{1,0:T(8,128)(2,1)S(1)}, u32[]{:S(2)}, u32[]{:S(2)}) collective-permute-start(bf16[128,1536]{1,0:T(8,128)(2,1)} %collective-permute-done.refs_2_), channel_id=1, source_target_pairs={{0,2},{2,4},{4,6},{6,8},{8,10},{10,12},{12,14},{14,0},{1,3},{3,5},... | collective-permute-start | bytes 1179656 | tf_op jit(solution)/shard_map/ppermute | solution.py:349
  73.1 13.0 %collective-permute-start.9 = (bf16[160,1536]{1,0:T(8,128)(2,1)S(1)}, bf16[160,1536]{1,0:T(8,128)(2,1)S(1)}, u32[]{:S(2)}, u32[]{:S(2)}) collective-permute-start(bf16[160,1536]{1,0:T(8,128)(2,1)S(1)} %get-tuple-element.46), channel_id=1, source_target_pairs={{0,14},{2,0},{4,2},{6,4},{8,6},{10,8},{12,10},{14,12},{1,15},{3,1}... | collective-permute-start | bytes 1474568 | tf_op jit(solution)/shard_map/ppermute | solution.py:349
  74.6 14.7 %collective-permute-start.13 = (bf16[160,1536]{1,0:T(8,128)(2,1)S(1)}, bf16[160,1536]{1,0:T(8,128)(2,1)S(1)}, u32[]{:S(2)}, u32[]{:S(2)}) collective-permute-start(bf16[160,1536]{1,0:T(8,128)(2,1)S(1)} %get-tuple-element.45), channel_id=1, source_target_pairs={{0,2},{2,4},{4,6},{6,8},{8,10},{10,12},{12,14},{14,0},{1,3},{3,5},... | collective-permute-start | bytes 1474568 | tf_op jit(solution)/shard_map/ppermute | solution.py:349
  86.1 14.2 %collective-permute-start.10 = (bf16[160,1536]{1,0:T(8,128)(2,1)S(1)}, bf16[160,1536]{1,0:T(8,128)(2,1)S(1)}, u32[]{:S(2)}, u32[]{:S(2)}) collective-permute-start(bf16[160,1536]{1,0:T(8,128)(2,1)S(1)} %collective-permute-done.9.refs_3_.refs_4_), channel_id=1, source_target_pairs={{0,14},{2,0},{4,2},{6,4},{8,6},{10,8},{12,10},{14,12},{1,15},{3,1}... | collective-permute-start | bytes 1474568 | tf_op jit(solution)/shard_map/ppermute | solution.py:349
  89.3 14.8 %collective-permute-start.14 = (bf16[160,1536]{1,0:T(8,128)(2,1)S(1)}, bf16[160,1536]{1,0:T(8,128)(2,1)S(1)}, u32[]{:S(2)}, u32[]{:S(2)}) collective-permute-start(bf16[160,1536]{1,0:T(8,128)(2,1)S(1)} %collective-permute-done.13.refs_7_.refs_8_), channel_id=1, source_target_pairs={{0,2},{2,4},{4,6},{6,8},{8,10},{10,12},{12,14},{14,0},{1,3},{3,5},... | collective-permute-start | bytes 1474568 | tf_op jit(solution)/shard_map/ppermute | solution.py:349
  100.3 7.3 %collective-permute-start.16 = (bf16[32,1536]{1,0:T(8,128)(2,1)S(1)}, bf16[32,1536]{1,0:T(8,128)(2,1)S(1)}, u32[]{:S(2)}, u32[]{:S(2)}) collective-permute-start(bf16[32,1536]{1,0:T(8,128)(2,1)S(1)} %slice.33), channel_id=1, source_target_pairs={{0,14},{2,0},{4,2},{6,4},{8,6},{10,8},{12,10},{14,12},{1,15},{3,1}... | collective-permute-start | bytes 294920 | tf_op jit(solution)/shard_map/ppermute | solution.py:349
  104.1 7.1 %collective-permute-start.18 = (bf16[32,1536]{1,0:T(8,128)(2,1)S(1)}, bf16[32,1536]{1,0:T(8,128)(2,1)S(1)}, u32[]{:S(2)}, u32[]{:S(2)}) collective-permute-start(bf16[32,1536]{1,0:T(8,128)(2,1)S(1)} %slice.35), channel_id=1, source_target_pairs={{0,2},{2,4},{4,6},{6,8},{8,10},{10,12},{12,14},{14,0},{1,3},{3,5},... | collective-permute-start | bytes 294920 | tf_op jit(solution)/shard_map/ppermute | solution.py:349
  104.2 18.4 %collective-permute-start.11 = (bf16[64,1536]{1,0:T(8,128)(2,1)S(1)}, bf16[64,1536]{1,0:T(8,128)(2,1)S(1)}, u32[]{:S(2)}, u32[]{:S(2)}) collective-permute-start(bf16[64,1536]{1,0:T(8,128)(2,1)S(1)} %slice.31), channel_id=1, source_target_pairs={{0,14},{2,0},{4,2},{6,4},{8,6},{10,8},{12,10},{14,12},{1,15},{3,1}... | collective-permute-start | bytes 589832 | tf_op jit(solution)/shard_map/ppermute | solution.py:349
  107.6 15.1 %collective-permute-start.15 = (bf16[64,1536]{1,0:T(8,128)(2,1)S(1)}, bf16[64,1536]{1,0:T(8,128)(2,1)S(1)}, u32[]{:S(2)}, u32[]{:S(2)}) collective-permute-start(bf16[64,1536]{1,0:T(8,128)(2,1)S(1)} %slice.32), channel_id=1, source_target_pairs={{0,2},{2,4},{4,6},{6,8},{8,10},{10,12},{12,14},{14,0},{1,3},{3,5},... | collective-permute-start | bytes 589832 | tf_op jit(solution)/shard_map/ppermute | solution.py:349
  111.2 5.4 %collective-permute-start.19 = (bf16[16,1536]{1,0:T(8,128)(2,1)S(1)}, bf16[16,1536]{1,0:T(8,128)(2,1)S(1)}, u32[]{:S(2)}, u32[]{:S(2)}) collective-permute-start(bf16[16,1536]{1,0:T(8,128)(2,1)S(1)} %slice.36), channel_id=1, source_target_pairs={{0,2},{2,4},{4,6},{6,8},{8,10},{10,12},{12,14},{14,0},{1,3},{3,5},... | collective-permute-start | bytes 147464 | tf_op jit(solution)/shard_map/ppermute | solution.py:349
  124.1 46.4 %all-to-all-start.1 = ((bf16[16,384,128]{2,1,0:T(8,128)(2,1)}), bf16[16,384,128]{2,1,0:T(8,128)(2,1)S(1)}, u32[]{:S(2)}, u32[]{:S(2)}) async-start(bf16[16,384,128]{2,1,0:T(8,128)(2,1)} %after.6), calls=%async_computation.1 | async-start | bytes 3145728 | tf_op jit(solution)/shard_map/all_to_all | solution.py:473
  170.5 57.6 %all-to-all-start.2 = ((bf16[16,384,128]{2,1,0:T(8,128)(2,1)}), bf16[16,384,128]{2,1,0:T(8,128)(2,1)S(1)}, u32[]{:S(2)}, u32[]{:S(2)}) async-start(bf16[16,384,128]{2,1,0:T(8,128)(2,1)} %after.7), calls=%async_computation.2 | async-start | bytes 3145728 | tf_op jit(solution)/shard_map/all_to_all | solution.py:479
  174.2 13.5 %collective-permute-start.22 = (bf16[8,128,128]{2,1,0:T(8,128)(2,1)}, bf16[8,128,128]{2,1,0:T(8,128)(2,1)S(1)}, u32[]{:S(2)}, u32[]{:S(2)}) collective-permute-start(bf16[8,128,128]{2,1,0:T(8,128)(2,1)} %copy-done.43), channel_id=1, source_target_pairs={{0,0},{1,16},{16,1},{17,17},{2,2},{3,18},{18,3},{19,19},{4,4},{5,2... | collective-permute-start | bytes 786440 | tf_op jit(solution)/shard_map/ppermute | solution.py:386
  175.8 16.2 %collective-permute-start.23 = (bf16[8,128,128]{2,1,0:T(8,128)(2,1)S(1)}, bf16[8,128,128]{2,1,0:T(8,128)(2,1)S(1)}, u32[]{:S(2)}, u32[]{:S(2)}) collective-permute-start(bf16[8,128,128]{2,1,0:T(8,128)(2,1)S(1)} %copy-done.42), channel_id=1, source_target_pairs={{0,1},{1,17},{16,0},{17,16},{2,3},{3,19},{18,2},{19,18},{4,5},{5,2... | collective-permute-start | bytes 786440 | tf_op jit(solution)/shard_map/ppermute | solution.py:386
  229.3 65.5 %all-to-all-start.3 = ((bf16[16,384,128]{2,1,0:T(8,128)(2,1)}), bf16[16,384,128]{2,1,0:T(8,128)(2,1)S(1)}, u32[]{:S(2)}, u32[]{:S(2)}) async-start(bf16[16,384,128]{2,1,0:T(8,128)(2,1)} %after.8), calls=%async_computation.3 | async-start | bytes 3145728 | tf_op jit(solution)/shard_map/all_to_all | solution.py:485
  245.5 12.9 %collective-permute-start.24 = (bf16[8,128,128]{2,1,0:T(8,128)(2,1)}, bf16[8,128,128]{2,1,0:T(8,128)(2,1)S(1)}, u32[]{:S(2)}, u32[]{:S(2)}) collective-permute-start(bf16[8,128,128]{2,1,0:T(8,128)(2,1)} %copy-done.47), channel_id=1, source_target_pairs={{0,0},{16,1},{1,16},{17,17},{2,2},{18,3},{3,18},{19,19},{4,4},{20,... | collective-permute-start | bytes 786440 | tf_op jit(solution)/shard_map/ppermute | solution.py:386
  247.1 11.3 %collective-permute-start.25 = (bf16[8,128,128]{2,1,0:T(8,128)(2,1)}, bf16[8,128,128]{2,1,0:T(8,128)(2,1)}, u32[]{:S(2)}, u32[]{:S(2)}) collective-permute-start(bf16[8,128,128]{2,1,0:T(8,128)(2,1)} %copy-done.46), channel_id=1, source_target_pairs={{1,0},{17,1},{0,16},{16,17},{3,2},{19,3},{2,18},{18,19},{5,4},{21,... | collective-permute-start | bytes 786440 | tf_op jit(solution)/shard_map/ppermute | solution.py:386
  251.1 7.4 %collective-permute-start.27 = (bf16[8,32,128]{2,1,0:T(8,128)(2,1)}, bf16[8,32,128]{2,1,0:T(8,128)(2,1)S(1)}, u32[]{:S(2)}, u32[]{:S(2)}) collective-permute-start(bf16[8,32,128]{2,1,0:T(8,128)(2,1)} %copy-done.48), channel_id=1, source_target_pairs={{1,0},{17,1},{0,16},{16,17},{3,2},{19,3},{2,18},{18,19},{5,4},{21,... | collective-permute-start | bytes 196616 | tf_op jit(solution)/shard_map/ppermute | solution.py:386
  268.9 7.8 %collective-permute-start.29 = (f32[2,2,8,1536]{3,2,1,0:T(8,128)S(1)}, f32[2,2,8,1536]{3,2,1,0:T(8,128)S(1)}, u32[]{:S(2)}, u32[]{:S(2)}) collective-permute-start(f32[2,2,8,1536]{3,2,1,0:T(8,128)S(1)} %get-tuple-element.34), channel_id=1, source_target_pairs={{0,32},{32,64},{64,96},{96,0},{1,33},{33,65},{65,97},{97,1},{2,34}... | collective-permute-start | bytes 589832 | tf_op jit(solution)/shard_map/ppermute | solution.py:349
  270.5 9.3 %collective-permute-start.30 = (f32[2,2,8,1536]{3,2,1,0:T(8,128)S(1)}, f32[2,2,8,1536]{3,2,1,0:T(8,128)S(1)}, u32[]{:S(2)}, u32[]{:S(2)}) collective-permute-start(f32[2,2,8,1536]{3,2,1,0:T(8,128)S(1)} %get-tuple-element.36), channel_id=1, source_target_pairs={{0,64},{32,96},{64,0},{96,32},{1,65},{33,97},{65,1},{97,33},{2,66}... | collective-permute-start | bytes 589832 | tf_op jit(solution)/shard_map/ppermute | solution.py:349
  271.6 10.6 %collective-permute-start.31 = (f32[2,2,8,1536]{3,2,1,0:T(8,128)S(1)}, f32[2,2,8,1536]{3,2,1,0:T(8,128)S(1)}, u32[]{:S(2)}, u32[]{:S(2)}) collective-permute-start(f32[2,2,8,1536]{3,2,1,0:T(8,128)S(1)} %get-tuple-element.35), channel_id=1, source_target_pairs={{0,96},{32,0},{64,32},{96,64},{1,97},{33,1},{65,33},{97,65},{2,98}... | collective-permute-start | bytes 589832 | tf_op jit(solution)/shard_map/ppermute | solution.py:349
  282.2 6.5 %collective-permute-start.32 = (f32[8,1536]{1,0:T(8,128)S(1)}, f32[8,1536]{1,0:T(8,128)S(1)}, u32[]{:S(2)}, u32[]{:S(2)}) collective-permute-start(f32[8,1536]{1,0:T(8,128)S(1)} %get-tuple-element.42), channel_id=1, source_target_pairs={{0,0},{1,16},{16,1},{17,17},{128,128},{129,144},{144,129},{145,145... | collective-permute-start | bytes 147464 | tf_op jit(solution)/shard_map/ppermute | solution.py:444
  282.9 5.9 %collective-permute-start.33 = (f32[8,1536]{1,0:T(8,128)S(1)}, f32[8,1536]{1,0:T(8,128)S(1)}, u32[]{:S(2)}, u32[]{:S(2)}) collective-permute-start(f32[8,1536]{1,0:T(8,128)S(1)} %get-tuple-element.39), channel_id=1, source_target_pairs={{0,16},{1,0},{16,17},{17,1},{128,144},{129,128},{144,145},{145,129... | collective-permute-start | bytes 147464 | tf_op jit(solution)/shard_map/ppermute | solution.py:444
  285.9 5.6 %collective-permute-start.34 = (f32[8,1536]{1,0:T(8,128)S(1)}, f32[8,1536]{1,0:T(8,128)S(1)}, u32[]{:S(2)}, u32[]{:S(2)}) collective-permute-start(f32[8,1536]{1,0:T(8,128)S(1)} %get-tuple-element.41), channel_id=1, source_target_pairs={{0,128},{1,144},{16,129},{17,145},{128,0},{129,16},{144,1},{145,17... | collective-permute-start | bytes 147464 | tf_op jit(solution)/shard_map/ppermute | solution.py:444
  (59 other events, 465.9 us)
